TPU v7x, 256 devices: a whole 4x4x8 slice. The times are simulated.
256 devices in a mesh: seq: 16 (over z, core), clip: 16 (over y, x).
Axes of the slice: x: 4, y: 4, z: 8, core: 2. Of those that a mesh axis runs over, the one named last changes fastest.
Arguments:
- qkv: bfloat16 [16, 2048, 4224], P('clip', 'seq'), may hold values from -6 to 6
- w_out: bfloat16 [1408, 1408], replicated, may hold values from -0.15625 to 0.15625
- enc_gain: float32 [1408], replicated, may hold values from 0.5 to 1.5
- w_embed: bfloat16 [1408, 384], replicated, may hold values from -0.15625 to 0.15625
- pred_gain: float32 [384], replicated, may hold values from 0.5 to 1.5
- ctx_blocks: int32 [192, 12], replicated, may hold values from 0 to 15, as said below
- owner: int32 [192], replicated, may hold values from 0 to 15, as said below
- cotangent: bfloat16 [16, 16, 16, 128, 384], P('clip', 'seq'), may hold values from -6 to 6
Outputs:
- prediction: bfloat16 [16, 16, 16, 128, 384], P('clip', 'seq')
- qkv_grad: bfloat16 [16, 2048, 4224], P('clip', 'seq')
Inputs may be any that keep to these rules, and one draw needn't show every extreme that they name: `ctx_blocks`: the 12 blocks of one mask are distinct. `owner`: the 12 masks of one clip have distinct owners.
All inputs are finite; a program needn't handle non-finite values.
Results may differ from a plain program's by a relative error of at most 0.025.
Values may be sent and summed in bfloat16 or wider, within the bound.
A program may use at most 128 MiB of HBM per device.

v0:
```python
import jax
import jax.numpy as jnp
from jax import lax
from jax.sharding import PartitionSpec as P

E = 88


epsilon = 1e-06
contract_last = (((1,), (1,)), ((), ()))
contract_first = (((0,), (0,)), ((), ()))


def norm_forward(values, scaling_gain):
    average = jnp.mean(values, axis=-1, keepdims=True)
    centred = values - average
    variance = jnp.mean(centred * centred, axis=-1, keepdims=True)
    inverse = lax.rsqrt(variance + epsilon)
    normed = centred * inverse
    return (normed * scaling_gain, normed, inverse)


def norm_backward(normed, inverse, upstream):
    average_one = jnp.mean(upstream, axis=-1, keepdims=True)
    average_two = jnp.mean(upstream * normed, axis=-1, keepdims=True)
    return inverse * (upstream - average_one - normed * average_two)


def mask_table(ctx_blocks, owner, clip_count, shard_count):
    mask_count = owner.shape[0]
    clip_of = jnp.arange(mask_count, dtype=jnp.int32) // (mask_count // clip_count)
    member = jnp.any(
        ctx_blocks[:, :, None] == jnp.arange(shard_count, dtype=jnp.int32)[None, None, :], axis=1
    )
    in_clip = clip_of[:, None] == jnp.arange(clip_count, dtype=jnp.int32)[None, :]
    owned_by = owner[:, None] == jnp.arange(clip_count, dtype=jnp.int32)[None, :]
    return jnp.einsum(
        "mc,ms,mo->cso",
        in_clip.astype(jnp.float32),
        member.astype(jnp.float32),
        owned_by.astype(jnp.float32),
    )


def to_heads(token_rows):
    number = lax.axis_size("seq")
    columns_each = token_rows.shape[1] // number
    regrouped = lax.all_to_all(
        token_rows.reshape(token_rows.shape[0], number, columns_each),
        "seq",
        split_axis=1,
        concat_axis=0,
        tiled=True,
    )
    return regrouped.reshape(regrouped.shape[0], columns_each)


def to_rows(head_columns):
    number = lax.axis_size("seq")
    regrouped = lax.all_to_all(
        head_columns.reshape(head_columns.shape[0], 1, head_columns.shape[1]),
        "seq",
        split_axis=0,
        concat_axis=1,
        tiled=True,
    )
    return regrouped.reshape(regrouped.shape[0], number * head_columns.shape[1])


def block_weights(query_block, key_rows, scaling):
    scores = (
        lax.dot_general(query_block, key_rows, contract_last, preferred_element_type=jnp.float32)
        * scaling
    )
    shifted = jnp.exp(scores - jnp.max(scores, axis=-1, keepdims=True))
    return shifted / jnp.sum(shifted, axis=-1, keepdims=True)


def head_forward(query_rows, key_rows, value_rows, block_rows):
    scaling = query_rows.shape[-1] ** (-0.5)

    def one_block(query_block):
        weights_low = block_weights(query_block, key_rows, scaling).astype(jnp.bfloat16)
        return jnp.dot(weights_low, value_rows, preferred_element_type=jnp.float32).astype(
            jnp.bfloat16
        )

    stacked = query_rows.reshape(query_rows.shape[0] // block_rows, block_rows, query_rows.shape[1])
    return lax.map(one_block, stacked).reshape(query_rows.shape)


def head_backward(query_rows, key_rows, value_rows, output_rows, grad_out, block_rows):
    scaling = query_rows.shape[-1] ** (-0.5)
    number = query_rows.shape[0] // block_rows
    columns_each = query_rows.shape[1]

    def one_block(totals, inputs):
        query_block, output_block, grad_block = inputs
        weights = block_weights(query_block, key_rows, scaling)
        weights_low = weights.astype(jnp.bfloat16)
        grad_value = totals[0] + lax.dot_general(
            weights_low, grad_block, contract_first, preferred_element_type=jnp.float32
        )
        grad_weights = lax.dot_general(
            grad_block, value_rows, contract_last, preferred_element_type=jnp.float32
        )
        correction = jnp.sum(
            grad_block.astype(jnp.float32) * output_block.astype(jnp.float32),
            axis=-1,
            keepdims=True,
        )
        grad_scores = (weights * (grad_weights - correction) * scaling).astype(jnp.bfloat16)
        grad_query = jnp.dot(grad_scores, key_rows, preferred_element_type=jnp.float32).astype(
            jnp.bfloat16
        )
        grad_key = totals[1] + lax.dot_general(
            grad_scores, query_block, contract_first, preferred_element_type=jnp.float32
        )
        return ((grad_value, grad_key), grad_query)

    empty_sum = jnp.zeros(key_rows.shape, jnp.float32)
    shaped = (
        query_rows.reshape(number, block_rows, columns_each),
        output_rows.reshape(number, block_rows, columns_each),
        grad_out.reshape(number, block_rows, columns_each),
    )
    (grad_value, grad_key), grad_query = lax.scan(one_block, (empty_sum, empty_sum), shaped)
    return (
        grad_query.reshape(query_rows.shape),
        grad_key.astype(jnp.bfloat16),
        grad_value.astype(jnp.bfloat16),
    )


def on_device(qkv, w_out, enc_gain, w_embed, pred_gain, ctx_blocks, owner, cotangent):
    clip_count = lax.axis_size("clip")
    shard_count = lax.axis_size("seq")
    my_clip = lax.axis_index("clip")
    my_shard = lax.axis_index("seq")
    rows_local = qkv.shape[1]
    local_heads = to_heads(qkv[0])
    sequence = local_heads.shape[0]
    heads_here = local_heads.shape[1] // (3 * E)
    block_rows = min(512, sequence)
    per_head = local_heads.reshape(sequence, heads_here, 3, E)
    outputs = [head_forward(per_head[:, 0, 0], per_head[:, 0, 1], per_head[:, 0, 2], block_rows)]
    heads_out = jnp.stack(outputs, axis=1).reshape(sequence, heads_here * E)
    token_rows = to_rows(heads_out)
    encoded = jnp.dot(token_rows, w_out, preferred_element_type=jnp.float32)
    context, normed_enc, inverse_enc = norm_forward(encoded, enc_gain)
    context = context.astype(jnp.bfloat16)
    embedded = jnp.dot(context, w_embed, preferred_element_type=jnp.float32)
    predicted, normed_emb, inverse_emb = norm_forward(embedded, pred_gain)
    predicted = predicted.astype(jnp.bfloat16)
    routing = mask_table(ctx_blocks, owner, clip_count, shard_count)
    sending = routing[my_clip, my_shard] > 0.5
    outgoing = jnp.where(sending[:, None, None], context[None], 0)
    landed = lax.all_to_all(outgoing, "clip", split_axis=0, concat_axis=0, tiled=True)
    slot_embedded = jnp.dot(
        landed.reshape(clip_count * rows_local, landed.shape[2]),
        w_embed,
        preferred_element_type=jnp.float32,
    )
    arrived = (
        norm_forward(slot_embedded, pred_gain)[0]
        .astype(jnp.bfloat16)
        .reshape(clip_count, rows_local, slot_embedded.shape[1])
    )
    prediction = arrived[None, None]
    slot_rows = cotangent[0, 0]
    returned = lax.all_to_all(slot_rows, "clip", split_axis=0, concat_axis=0, tiled=True)
    grad_predicted = jnp.einsum(
        "o,obp->bp", sending.astype(jnp.bfloat16), returned, preferred_element_type=jnp.float32
    )
    grad_embedded = norm_backward(normed_emb, inverse_emb, grad_predicted * pred_gain).astype(
        jnp.bfloat16
    )
    grad_context = lax.dot_general(
        grad_embedded, w_embed, contract_last, preferred_element_type=jnp.float32
    )
    grad_encoded = norm_backward(normed_enc, inverse_enc, grad_context * enc_gain).astype(
        jnp.bfloat16
    )
    grad_rows = lax.dot_general(
        grad_encoded, w_out, contract_last, preferred_element_type=jnp.float32
    ).astype(jnp.bfloat16)
    grad_heads = to_heads(grad_rows).reshape(sequence, heads_here, E)
    grad_query, grad_key, grad_value = head_backward(
        per_head[:, 0, 0],
        per_head[:, 0, 1],
        per_head[:, 0, 2],
        outputs[0],
        grad_heads[:, 0],
        block_rows,
    )
    gathered_grads = [jnp.stack([grad_query, grad_key, grad_value], axis=1)]
    grads_local = jnp.stack(gathered_grads, axis=1).reshape(sequence, heads_here * 3 * E)
    qkv_grad = to_rows(grads_local)
    return (prediction, qkv_grad[None])


def solution(mesh):
    placed = (
        P("clip", "seq", None),
        P(),
        P(),
        P(),
        P(),
        P(),
        P(),
        P("clip", "seq", None, None, None),
    )
    return jax.shard_map(
        on_device,
        mesh=mesh,
        in_specs=placed,
        out_specs=(P("clip", "seq", None, None, None), P("clip", "seq", None)),
        check_vma=False,
    )
```

profile of v0, /device:TPU:1, one launch (start us, length us, event | category | flops | bytes accessed | tf_op | source)
XLA Modules:
  0.0 306.2 jit_solution(442149951351988637)
XLA Ops:
  0.7 2.4 copy.69
  3.1 10.0 %all-to-all-start = ((bf16[128,16,264]{0,2,1:T(8,128)(2,1)}), bf16[128,16,264]{0,2,1:T(8,128)(2,1)S(1)}, u32[]{:S(2)}, u32[]{:S(2)}) async-start(bf16[128,16,264]{0,2,1:T(8,128)(2,1)} %bitcast.4), calls=%async_computation | async-start | bytes 2162688 | tf_op jit(solution)/shard_map/all_to_all | solution.py:48
  13.1 28.5 %all-to-all-done = bf16[128,16,264]{0,2,1:T(8,128)(2,1)S(1)} async-done(((bf16[128,16,264]{0,2,1:T(8,128)(2,1)}), bf16[128,16,264]{0,2,1:T(8,128)(2,1)S(1)}, u32[]{:S(2)}, u32[]{:S(2)}) %all-to-all-start) | async-done | bytes 1081376 | tf_op jit(solution)/shard_map/all_to_all | solution.py:48
  41.7 6.8 %all-to-all-start.3 = ((bf16[16,128,384]{2,1,0:T(8,128)(2,1)}), bf16[16,128,384]{2,1,0:T(8,128)(2,1)}, u32[]{:S(2)}, u32[]{:S(2)}) async-start(bf16[16,128,384]{2,1,0:T(8,128)(2,1)} %bitcast.149), calls=%async_computation.3 | async-start | bytes 3145728 | tf_op jit(solution)/shard_map/all_to_all | solution.py:171
  50.8 11.2 %while.25 = (s32[]{:T(128)}, bf16[4,512,88]{1,2,0:T(8,128)(2,1)S(1)}, bf16[4,512,88]{2,1,0:T(8,128)(2,1)S(1)}, bf16[2048,88]{1,0:T(8,128)(2,1)S(1)}, bf16[2048,88]{1,0:T(8,128)(2,1)}, /*index=5*/s32[]{:T(128)}) while((s32[]{:T(128)}, bf16[4,512,88]{1,2,0:T(8,128)(2,1)S(1)}, bf16[4,512,88]{2,1,0:T(8,128)(2,1)S(1)}, ...), condition=%wide.region_4.5_spmd, body=%wide.region_1.4_spmd.sunk | while | flops 378579968 | bytes 15304817 | solution.py:89
  64.5 12.5 %reduce = bf16[2048,88]{1,0:T(8,128)(2,1)S(1)} reduce(bf16[2048,1,88]{2,1,0:T(2,128)(2,1)} %reshape.111, bf16[]{:T(256)} %broadcast.193), dimensions={1}, to_apply=%reshape.111.reduce_sub_computation | reduce | bytes 720898 | tf_op jit(solution)/shard_map/stack;reshape | solution.py:147
  78.9 3.9 %all-to-all-start.1 = ((bf16[16,2,5632]{2,1,0:T(2,128)(2,1)}), bf16[16,2,5632]{2,1,0:T(2,128)(2,1)S(1)}, u32[]{:S(2)}, u32[]{:S(2)}) async-start(bf16[16,2,5632]{2,1,0:T(2,128)(2,1)} %reshape.112), calls=%async_computation.1 | async-start | bytes 720896 | tf_op jit(solution)/shard_map/all_to_all | solution.py:60
  82.9 2.4 fusion.30
  85.3 11.2 %all-to-all-done.1 = bf16[16,2,5632]{2,1,0:T(2,128)(2,1)S(1)} async-done(((bf16[16,2,5632]{2,1,0:T(2,128)(2,1)}), bf16[16,2,5632]{2,1,0:T(2,128)(2,1)S(1)}, u32[]{:S(2)}, u32[]{:S(2)}) %all-to-all-start.1) | async-done | bytes 360480 | tf_op jit(solution)/shard_map/all_to_all | solution.py:60
  96.5 2.9 reshape.113
  99.5 2.3 copy.76
  102.0 3.0 fusion.56
  110.0 4.1 %all-to-all-start.4 = ((bf16[128,16,88]{0,2,1:T(8,128)(2,1)}), bf16[128,16,88]{0,2,1:T(8,128)(2,1)}, u32[]{:S(2)}, u32[]{:S(2)}) async-start(bf16[128,16,88]{0,2,1:T(8,128)(2,1)} %bitcast.16), calls=%async_computation.4 | async-start | bytes 720896 | tf_op jit(solution)/shard_map/all_to_all | solution.py:48
  114.2 13.0 %all-to-all-done.4 = bf16[128,16,88]{0,2,1:T(8,128)(2,1)} async-done(((bf16[128,16,88]{0,2,1:T(8,128)(2,1)}), bf16[128,16,88]{0,2,1:T(8,128)(2,1)}, u32[]{:S(2)}, u32[]{:S(2)}) %all-to-all-start.4) | async-done | bytes 360480 | tf_op jit(solution)/shard_map/all_to_all | solution.py:48
  129.9 30.9 %while.26 = (s32[]{:T(128)}, f32[2048,88]{0,1:T(8,128)}, f32[2048,88]{0,1:T(8,128)S(1)}, bf16[4,512,88]{1,2,0:T(8,128)(2,1)}, bf16[4,512,88]{2,1,0:T(8,128)(2,1)...) while((s32[]{:T(128)}, f32[2048,88]{0,1:T(8,128)}, ...), condition=%wide.region_19.20_spmd.clone, body=%wide.region_15.19_spmd.clone.sunk | while | flops 940468736 | bytes 36825352 | solution.py:127
  167.6 3.5 %reshape.114 = bf16[16,2,16896]{2,1,0:T(2,128)(2,1)} reshape(bf16[2048,264]{1,0:T(8,128)(2,1)S(1)} %copy.111) | data formatting | bytes 2162688
  171.1 3.6 %all-to-all-start.5 = ((bf16[16,2,16896]{2,1,0:T(2,128)(2,1)}), bf16[16,2,16896]{2,1,0:T(2,128)(2,1)S(1)}, u32[]{:S(2)}, u32[]{:S(2)}) async-start(bf16[16,2,16896]{2,1,0:T(2,128)(2,1)} %reshape.114), calls=%async_computation.5 | async-start | bytes 2162688 | tf_op jit(solution)/shard_map/all_to_all | solution.py:60
  174.7 3.2 %broadcast_select_fusion = bf16[16,128,1408]{2,1,0:T(8,128)(2,1)} fusion(pred[16]{0:T(512)(128)(4,1)S(1)} %compare_bitcast_fusion, bf16[128,1408]{1,0:T(8,128)(2,1)S(1)} %copy-done.3), kind=kLoop, calls=%fused_computation.39 | loop fusion | flops 2883584 | bytes 6127632 | tf_op jit(solution)/shard_map/jit(_where)/select_n | solution.py:157
  177.9 24.6 %all-to-all-done.5 = bf16[16,2,16896]{2,1,0:T(2,128)(2,1)S(1)} async-done(((bf16[16,2,16896]{2,1,0:T(2,128)(2,1)}), bf16[16,2,16896]{2,1,0:T(2,128)(2,1)S(1)}, u32[]{:S(2)}, u32[]{:S(2)}) %all-to-all-start.5) | async-done | bytes 1081376 | tf_op jit(solution)/shard_map/all_to_all | solution.py:60
  202.5 7.0 %all-to-all-start.2 = ((bf16[16,128,1408]{2,1,0:T(8,128)(2,1)}), bf16[16,128,1408]{2,1,0:T(8,128)(2,1)}, u32[]{:S(2)}, u32[]{:S(2)}) async-start(bf16[16,128,1408]{2,1,0:T(8,128)(2,1)} %broadcast_select_fusion), calls=%async_computation.2 | async-start | bytes 11534336 | tf_op jit(solution)/shard_map/all_to_all | solution.py:158
  209.4 7.7 %reshape.115 = bf16[2048,1,264]{2,1,0:T(2,128)(2,1)} reshape(bf16[16,2,16896]{2,1,0:T(2,128)(2,1)S(1)} %all-to-all-done.5) | data formatting | bytes 2162688
  217.1 6.9 %copy.87 = bf16[2048,1,264]{0,2,1:T(8,128)(2,1)S(1)} copy(bf16[2048,1,264]{2,1,0:T(2,128)(2,1)} %reshape.115) | data formatting | bytes 2162688 | tf_op jit(solution)/shard_map/all_to_all | solution.py:60
  226.2 72.1 %all-to-all-done.2 = bf16[16,128,1408]{2,1,0:T(8,128)(2,1)} async-done(((bf16[16,128,1408]{2,1,0:T(8,128)(2,1)}), bf16[16,128,1408]{2,1,0:T(8,128)(2,1)}, u32[]{:S(2)}, u32[]{:S(2)}) %all-to-all-start.2) | async-done | bytes 5767200 | tf_op jit(solution)/shard_map/all_to_all | solution.py:158
  298.3 5.5 %fusion.57 = (f32[2048]{0:T(1024)S(1)}, f32[2048,384]{1,0:T(8,128)S(1)}) fusion(bf16[2048,1408]{1,0:T(8,128)(2,1)} %bitcast.11, bf16[1408,384]{1,0:T(8,128)(2,1)S(1)} %copy-done), kind=kOutput, calls=%fused_computation.103 | convolution fusion | flops 2215376896 | bytes 10002432 | tf_op jit(solution)/shard_map/dot_general | solution.py:159
  (149 shorter events, 67.3 us)
Async XLA Ops:
  0.6 105.6 %copy-start = (bf16[1408,384]{1,0:T(8,128)(2,1)S(1)}, bf16[1408,384]{1,0:T(8,128)(2,1)}, u32[]{:S(2)}) copy-start(bf16[1408,384]{1,0:T(8,128)(2,1)} %param.15) | copy-start | bytes 3244036
  0.6 12.4 %copy-start.11 = (s32[192,12]{0,1:T(8,128)S(1)}, s32[192,12]{0,1:T(8,128)}, u32[]{:S(2)}) copy-start(s32[192,12]{0,1:T(8,128)} %param.17) | copy-start | bytes 27652
  3.1 38.6 %all-to-all-start = ((bf16[128,16,264]{0,2,1:T(8,128)(2,1)}), bf16[128,16,264]{0,2,1:T(8,128)(2,1)S(1)}, u32[]{:S(2)}, u32[]{:S(2)}) async-start(bf16[128,16,264]{0,2,1:T(8,128)(2,1)} %bitcast.4), calls=%async_computation | async-start | bytes 2162688 | tf_op jit(solution)/shard_map/all_to_all | solution.py:48
  41.7 37.2 %all-to-all-start.3 = ((bf16[16,128,384]{2,1,0:T(8,128)(2,1)}), bf16[16,128,384]{2,1,0:T(8,128)(2,1)}, u32[]{:S(2)}, u32[]{:S(2)}) async-start(bf16[16,128,384]{2,1,0:T(8,128)(2,1)} %bitcast.149), calls=%async_computation.3 | async-start | bytes 3145728 | tf_op jit(solution)/shard_map/all_to_all | solution.py:171
  62.0 20.7 %copy-start.12 = (s32[192]{0:T(256)S(1)}, s32[192]{0:T(256)}, u32[]{:S(2)}) copy-start(s32[192]{0:T(256)} %param.18) | copy-start | bytes 2308
  78.9 17.7 %all-to-all-start.1 = ((bf16[16,2,5632]{2,1,0:T(2,128)(2,1)}), bf16[16,2,5632]{2,1,0:T(2,128)(2,1)S(1)}, u32[]{:S(2)}, u32[]{:S(2)}) async-start(bf16[16,2,5632]{2,1,0:T(2,128)(2,1)} %reshape.112), calls=%async_computation.1 | async-start | bytes 720896 | tf_op jit(solution)/shard_map/all_to_all | solution.py:60
  99.5 5.8 %copy-start.9 = (f32[1408]{0:T(1024)S(1)}, f32[1408]{0:T(1024)}, u32[]{:S(2)}) copy-start(f32[1408]{0:T(1024)} %param.14) | copy-start | bytes 16900
  102.0 4.9 %copy-start.10 = (f32[384]{0:T(512)S(1)}, f32[384]{0:T(512)}, u32[]{:S(2)}) copy-start(f32[384]{0:T(512)} %param.16) | copy-start | bytes 4612
  105.0 2.7 copy-start.1
  110.0 17.2 %all-to-all-start.4 = ((bf16[128,16,88]{0,2,1:T(8,128)(2,1)}), bf16[128,16,88]{0,2,1:T(8,128)(2,1)}, u32[]{:S(2)}, u32[]{:S(2)}) async-start(bf16[128,16,88]{0,2,1:T(8,128)(2,1)} %bitcast.16), calls=%async_computation.4 | async-start | bytes 720896 | tf_op jit(solution)/shard_map/all_to_all | solution.py:48
  131.0 1.6 copy-start.4
  131.0 1.6 copy-start.5
  133.9 1.8 copy-start.6
  138.7 1.6 copy-start.4
  138.7 1.6 copy-start.5
  141.6 1.8 copy-start.6
  146.5 1.6 copy-start.4
  149.3 1.8 copy-start.6
  154.2 1.6 copy-start.4
  154.2 1.6 copy-start.5
  157.1 1.8 copy-start.6
  165.7 9.0 %copy-start.3 = (bf16[128,1408]{1,0:T(8,128)(2,1)S(1)}, bf16[128,1408]{1,0:T(8,128)(2,1)}, u32[]{:S(2)}) copy-start(bf16[128,1408]{1,0:T(8,128)(2,1)} %copy-done.2) | copy-start | bytes 1081348
  171.1 31.4 %all-to-all-start.5 = ((bf16[16,2,16896]{2,1,0:T(2,128)(2,1)}), bf16[16,2,16896]{2,1,0:T(2,128)(2,1)S(1)}, u32[]{:S(2)}, u32[]{:S(2)}) async-start(bf16[16,2,16896]{2,1,0:T(2,128)(2,1)} %reshape.114), calls=%async_computation.5 | async-start | bytes 2162688 | tf_op jit(solution)/shard_map/all_to_all | solution.py:60
  202.5 95.8 %all-to-all-start.2 = ((bf16[16,128,1408]{2,1,0:T(8,128)(2,1)}), bf16[16,128,1408]{2,1,0:T(8,128)(2,1)}, u32[]{:S(2)}, u32[]{:S(2)}) async-start(bf16[16,128,1408]{2,1,0:T(8,128)(2,1)} %broadcast_select_fusion), calls=%async_computation.2 | async-start | bytes 11534336 | tf_op jit(solution)/shard_map/all_to_all | solution.py:158
  (10 other events, 13.7 us)
where the time goes:
time: 307 us; the launch traced here: 306 us
  waiting for transfers between devices  150 us (49%)
  matrix products  44.3 us (14%)
  local copies, waits for them, and re-layouts  42.4 us (14%)
  starting transfers between devices  35.3 us (11%)
  other arithmetic  33.1 us (11%)
    all_to_all x1, waiting for transfers between devices, on_device(): lax.all_to_all(outgoing, 'clip', split_axis=0, concat_axis=0, tiled=True)  72.1 us
    all_to_all x2, waiting for transfers between devices, to_heads(): lax.all_to_all(token_rows.reshape(token_rows.shape[0], number, columns_ea...  41.6 us
    all_to_all x2, waiting for transfers between devices, to_rows(): lax.all_to_all(head_columns.reshape(head_columns.shape[0], 1, head_column...  35.8 us
    unnamed x26, local copies, waits for them, and re-layouts  24.9 us
    all_to_all x2, starting transfers between devices, to_heads(): lax.all_to_all(token_rows.reshape(token_rows.shape[0], number, columns_ea...  14.1 us
    another operation x1, other arithmetic, on_device(): heads_out = jnp.stack(outputs, axis=1).reshape(sequence, heads_here * E)  12.5 us
    all_to_all x4, local copies, waits for them, and re-layouts, to_rows(): lax.all_to_all(head_columns.reshape(head_columns.shape[0], 1, head_column...  9.57 us
    all_to_all x2, starting transfers between devices, to_rows(): lax.all_to_all(head_columns.reshape(head_columns.shape[0], 1, head_column...  7.45 us
  transfers between devices with their start and end apart: 6, of which 5 were waited for; matrix products, arithmetic and copies ran while one was open for 17% of the time, Pallas kernels for 0%

commit v1 on v0

v1 whole, which is shorter than its diff:
```python
import functools

import jax
import jax.numpy as jnp
from jax import lax
from jax.experimental import pallas as pl
from jax.experimental.pallas import tpu as pltpu
from jax.sharding import PartitionSpec as P

E = 88
EP = 96
L = 128
epsilon = 1e-06
MESH = pl.DeviceIdType.MESH
bf16, f32 = jnp.bfloat16, jnp.float32
contract_last = (((1,), (1,)), ((), ()))

KV, Q, HEADS, GRADS, DKV, DQ = range(6)
COT, PRED = range(2)


def dot(a, b):
    return jnp.dot(a, b, preferred_element_type=f32)


def dot_last(a, b):
    return lax.dot_general(a, b, contract_last, preferred_element_type=f32)


def block(index, size=L):
    return pl.ds(pl.multiple_of(index * size, size), size)


def normalize(values):
    average = jnp.mean(values, axis=-1, keepdims=True)
    centred = values - average
    variance = jnp.mean(centred * centred, axis=-1, keepdims=True)
    inverse = lax.rsqrt(variance + epsilon)
    return centred * inverse, inverse


def norm_backward(normed, inverse, upstream):
    average_one = jnp.mean(upstream, axis=-1, keepdims=True)
    average_two = jnp.mean(upstream * normed, axis=-1, keepdims=True)
    return inverse * (upstream - average_one - normed * average_two)


def rows_to(values, rows):
    return jnp.concatenate([values, jnp.zeros((rows - values.shape[0], values.shape[1]), values.dtype)])


def kernel(
    ns,
    nc,
    qkv,
    w_out_hbm,
    enc_gain,
    w_embed,
    pred_gain,
    ctx_blocks,
    owner,
    cot_hbm,
    prediction,
    qkv_grad,
    xt,
    w_out,
    kv_send,
    q_send,
    kvt,
    qt,
    kn,
    vn,
    qn,
    pt,
    ot,
    heads_recv,
    heads_rows,
    cot_recv,
    pred_send,
    pred_recv,
    grads_send,
    dot_t,
    dot_n,
    dq,
    dkv_send,
    dq_send,
    dkv_recv,
    dq_recv,
    seq_send_sem,
    seq_recv_sem,
    clip_send_sem,
    clip_recv_sem,
    local_sem,
):
    me = lax.axis_index("seq")
    clip = lax.axis_index("clip")
    pairs = ns // 2
    my_pair = lax.div(me, 2)
    partner = me + 1 - 2 * lax.rem(me, 2)
    d = ns * E
    tiles = d // L
    scaling = E**-0.5
    to_exp2 = scaling * 1.4426950408889634

    def seq_copy(phase, src, dst, peer):
        return pltpu.make_async_remote_copy(
            src_ref=src,
            dst_ref=dst,
            send_sem=seq_send_sem.at[phase, peer],
            recv_sem=seq_recv_sem.at[phase, me],
            device_id={"seq": peer},
            device_id_type=MESH,
        )

    def seq_wait(phase, dst, source):
        pltpu.make_async_remote_copy(
            src_ref=dst,
            dst_ref=dst,
            send_sem=seq_send_sem.at[phase, source],
            recv_sem=seq_recv_sem.at[phase, source],
            device_id={"seq": source},
            device_id_type=MESH,
        ).wait_recv()

    def clip_copy(phase, src, dst, peer):
        return pltpu.make_async_remote_copy(
            src_ref=src,
            dst_ref=dst,
            send_sem=clip_send_sem.at[phase, peer],
            recv_sem=clip_recv_sem.at[phase, clip],
            device_id={"clip": peer},
            device_id_type=MESH,
        )

    def clip_wait(phase, dst, source):
        pltpu.make_async_remote_copy(
            src_ref=dst,
            dst_ref=dst,
            send_sem=clip_send_sem.at[phase, source],
            recv_sem=clip_recv_sem.at[phase, source],
            device_id={"clip": source},
            device_id_type=MESH,
        ).wait_recv()

    def seq_at(offset):
        return lax.rem(me + offset + ns, ns)

    def clip_at(offset):
        return lax.rem(clip + offset + nc, nc)

    def each(first, last, body):
        def step(i, carry):
            body(i)
            return carry

        lax.fori_loop(first, last, step, 0)

    barrier = pltpu.get_barrier_semaphore()
    each(1, ns, lambda j: pl.semaphore_signal(barrier, inc=1, device_id={"seq": seq_at(j)}, device_id_type=MESH))
    each(1, nc, lambda j: pl.semaphore_signal(barrier, inc=1, device_id={"clip": clip_at(j)}, device_id_type=MESH))

    w_out_copy = pltpu.make_async_copy(w_out_hbm, w_out, local_sem.at[0])
    w_out_copy.start()
    own_cot = pltpu.make_async_copy(cot_hbm.at[0, 0, clip], cot_recv.at[clip], local_sem.at[1])
    own_cot.start()

    for j in range(3 * tiles):
        xt[j * L : (j + 1) * L, :] = qkv[0, :, j * L : (j + 1) * L].astype(f32).T

    def cut(h):
        first = 3 * E * h
        kv_send[h] = xt[pl.ds(pl.multiple_of(first + E, 8), 2 * E), :].astype(bf16)
        q_send[h] = xt[pl.ds(pl.multiple_of(first, 8), EP), :].astype(bf16)

    each(0, ns, cut)
    pl.semaphore_wait(barrier, ns + nc - 2)

    def send_kv(j):
        peer = seq_at(j)
        seq_copy(KV, kv_send.at[peer], kvt.at[:, block(me)], peer).start()

    def send_q(j):
        peer = seq_at(j)
        seq_copy(Q, q_send.at[peer], qt.at[pl.ds(0, EP), block(me)], peer).start()

    def send_cot(j):
        peer = clip_at(j)
        clip_copy(COT, cot_hbm.at[0, 0, peer], cot_recv.at[clip], peer).start()

    each(1, ns, send_kv)
    each(1, ns, send_q)
    each(1, nc, send_cot)

    kvt[:, block(me)] = kv_send[me]
    qt[pl.ds(0, EP), block(me)] = q_send[me]
    qt[pl.ds(EP, L - EP), :] = jnp.zeros((L - EP, ns * L), bf16)
    dot_t[pl.ds(EP, L - EP), :] = jnp.zeros((L - EP, ns * L), bf16)
    dq[...] = jnp.zeros_like(dq)
    masks = owner.shape[1]
    per_clip = masks // nc
    owned = (lax.broadcasted_iota(jnp.int32, (nc, masks), 0) == owner[...]).astype(f32)
    member = jnp.max((ctx_blocks[...] == me).astype(f32), axis=1, keepdims=True)
    mask_id = lax.broadcasted_iota(jnp.int32, (masks, nc), 0)
    first_mask = lax.broadcasted_iota(jnp.int32, (masks, nc), 1) * per_clip
    in_clip = jnp.where((mask_id >= first_mask) & (mask_id < first_mask + per_clip), 1.0, 0.0)
    table = dot(owned, member * in_clip)
    sending = jnp.sum(
        jnp.where(lax.broadcasted_iota(jnp.int32, (nc, nc), 1) == clip, table, 0.0), axis=1, keepdims=True
    )
    receiving = jnp.sum(
        jnp.where(lax.broadcasted_iota(jnp.int32, (nc, nc), 0) == clip, table, 0.0), axis=0, keepdims=True
    )

    def turn_kv(source):
        both = kvt[:, block(source)].astype(f32)
        kn[block(source), :] = rows_to(both[:E], L).T.astype(bf16)
        vn[block(source), :] = rows_to(both[E:], L).T.astype(bf16)

    turn_kv(me)

    def take_kv(j):
        source = seq_at(-j)
        seq_wait(KV, kvt.at[:, block(source)], source)
        turn_kv(source)

    each(1, ns, take_kv)

    def turn_q(source):
        qn[block(source), :] = qt[:, block(source)].astype(f32).T.astype(bf16)

    def attend(pair):
        columns = block(pair, 2 * L)
        scores = dot(kn[...], qt[:, columns])
        shifted = jnp.exp2((scores - jnp.max(scores, axis=0, keepdims=True)) * to_exp2)
        probs = (shifted * (1.0 / jnp.sum(shifted, axis=0, keepdims=True))).astype(bf16)
        pt[:, columns] = probs
        mixed = dot(kvt[2 * E - EP :, :], probs)[EP - E :]
        ot[:, columns] = rows_to(mixed, EP).astype(bf16)

    def wait_q(source):
        seq_wait(Q, qt.at[pl.ds(0, EP), block(source)], source)

    def send_heads(peer):
        seq_copy(HEADS, ot.at[:, block(peer)], heads_recv.at[me], peer).start()

    wait_q(partner)
    attend(my_pair)
    send_heads(partner)
    heads_recv[me] = ot[:, block(me)]
    turn_q(me)
    turn_q(partner)

    def attend_far(i):
        pair = lax.rem(my_pair - i + pairs, pairs)
        wait_q(2 * pair)
        wait_q(2 * pair + 1)
        attend(pair)
        send_heads(2 * pair)
        send_heads(2 * pair + 1)
        turn_q(2 * pair)
        turn_q(2 * pair + 1)

    each(1, pairs, attend_far)

    own_cot.wait()
    each(1, nc, lambda j: clip_wait(COT, cot_recv.at[clip_at(-j)], clip_at(-j)))
    grad_predicted = jnp.zeros((L, cot_recv.shape[2]), f32)
    for o in range(nc):
        grad_predicted += sending[o : o + 1, :] * cot_recv[o].astype(f32)
    w_out_copy.wait()

    def take_heads(j):
        source = seq_at(-j)
        seq_wait(HEADS, heads_recv.at[source], source)

    each(1, ns, take_heads)
    for h in range(ns):
        xt[h * E : (h + 1) * E, :] = heads_recv[h].astype(f32)[:E]
    for j in range(tiles):
        heads_rows[:, j * L : (j + 1) * L] = xt[j * L : (j + 1) * L, :].T.astype(bf16)
    encoded = dot(heads_rows[...], w_out[...])
    normed_enc, inverse_enc = normalize(encoded)
    context = (normed_enc * enc_gain[...]).astype(bf16)
    embedded = dot(context, w_embed[...])
    normed_emb, inverse_emb = normalize(embedded)
    predicted = (normed_emb * pred_gain[...]).astype(bf16)
    pred_send[...] = predicted

    def send_pred(j):
        peer = clip_at(j)
        clip_copy(PRED, pred_send, pred_recv.at[clip], peer).start()

    grad_embedded = norm_backward(normed_emb, inverse_emb, grad_predicted * pred_gain[...]).astype(bf16)
    grad_context = dot_last(grad_embedded, w_embed[...])
    grad_encoded = norm_backward(normed_enc, inverse_enc, grad_context * enc_gain[...]).astype(bf16)
    xt[0:d, :] = dot_last(w_out[...], grad_encoded)

    def cut_grads(j):
        peer = seq_at(j)
        grads_send[peer] = xt[pl.ds(pl.multiple_of(peer * E, 8), EP), :].astype(bf16)
        seq_copy(GRADS, grads_send.at[peer], dot_t.at[pl.ds(0, EP), block(me)], peer).start()

    each(1, ns, cut_grads)
    each(1, nc, send_pred)
    dot_t[pl.ds(0, EP), block(me)] = xt[pl.ds(pl.multiple_of(me * E, 8), EP), :].astype(bf16)
    pred_recv[clip] = predicted

    def turn_grads(source):
        dot_n[block(source), :] = dot_t[:, block(source)].astype(f32).T.astype(bf16)

    turn_grads(me)

    def take_grads(j):
        source = seq_at(-j)
        seq_wait(GRADS, dot_t.at[pl.ds(0, EP), block(source)], source)
        turn_grads(source)

    each(1, ns, take_grads)

    correction = jnp.sum(dot_t[0:EP, :].astype(f32) * ot[...].astype(f32), axis=0, keepdims=True)

    def backward(pair):
        rows = block(pair, 2 * L)
        probs = pt[rows, :]
        grad_probs = dot(vn[rows, :], dot_t[...])
        grad_scores = (probs.astype(f32) * (grad_probs - correction)).astype(bf16)
        grad_value = dot(probs, dot_n[...])
        grad_key = dot(grad_scores, qn[...]) * scaling
        dq[...] += dot(kvt[0:EP, rows], grad_scores)
        dkv_send[:, rows] = jnp.concatenate([grad_key.T[:E], grad_value.T[:E]]).astype(bf16)

    def send_dkv(peer):
        seq_copy(DKV, dkv_send.at[:, block(peer)], dkv_recv.at[me], peer).start()

    def backward_far(i):
        pair = lax.rem(my_pair + i, pairs)
        backward(pair)
        send_dkv(2 * pair)
        send_dkv(2 * pair + 1)

    each(1, pairs, backward_far)
    backward(my_pair)
    send_dkv(partner)
    dkv_recv[me] = dkv_send[:, block(me)]
    dq_send[...] = (dq[...] * scaling).astype(bf16)

    def send_dq(j):
        peer = seq_at(j)
        seq_copy(DQ, dq_send.at[:, block(peer)], dq_recv.at[me], peer).start()

    each(1, ns, send_dq)
    dq_recv[me] = dq_send[:, block(me)]

    each(1, nc, lambda j: clip_wait(PRED, pred_recv.at[clip_at(-j)], clip_at(-j)))
    for c in range(nc):
        prediction[0, 0, c] = (pred_recv[c].astype(f32) * receiving[:, c : c + 1]).astype(bf16)

    def take_grad(j):
        source = seq_at(-j)
        seq_wait(DKV, dkv_recv.at[source], source)
        seq_wait(DQ, dq_recv.at[source], source)

    each(1, ns, take_grad)

    def place(h):
        first = 3 * E * h
        xt[pl.ds(pl.multiple_of(first, 8), E), :] = dq_recv[h].astype(f32)[:E]
        xt[pl.ds(pl.multiple_of(first + E, 8), 2 * E), :] = dkv_recv[h].astype(f32)

    each(0, ns, place)
    for j in range(3 * tiles):
        qkv_grad[0, :, j * L : (j + 1) * L] = xt[j * L : (j + 1) * L, :].T.astype(bf16)

    def sent(j):
        peer = seq_at(j)
        seq_copy(KV, kv_send.at[peer], kvt.at[:, block(me)], peer).wait_send()
        seq_copy(Q, q_send.at[peer], qt.at[pl.ds(0, EP), block(me)], peer).wait_send()
        seq_copy(HEADS, ot.at[:, block(peer)], heads_recv.at[me], peer).wait_send()
        seq_copy(GRADS, grads_send.at[peer], dot_t.at[pl.ds(0, EP), block(me)], peer).wait_send()
        seq_copy(DKV, dkv_send.at[:, block(peer)], dkv_recv.at[me], peer).wait_send()
        seq_copy(DQ, dq_send.at[:, block(peer)], dq_recv.at[me], peer).wait_send()

    def sent_clip(j):
        peer = clip_at(j)
        clip_copy(COT, cot_hbm.at[0, 0, peer], cot_recv.at[clip], peer).wait_send()
        clip_copy(PRED, pred_send, pred_recv.at[clip], peer).wait_send()

    each(1, ns, sent)
    each(1, nc, sent_clip)


def on_device(ns, nc, qkv, w_out, enc_gain, w_embed, pred_gain, ctx_blocks, owner, cotangent):
    d, width = w_embed.shape
    tokens = ns * L
    vmem = pl.BlockSpec(memory_space=pltpu.VMEM)
    hbm = pl.BlockSpec(memory_space=pl.ANY)
    scratch = [
        pltpu.VMEM((3 * d + 16, L), f32),
        pltpu.VMEM((d, d), bf16),
        pltpu.VMEM((ns, 2 * E, L), bf16),
        pltpu.VMEM((ns, EP, L), bf16),
        pltpu.VMEM((2 * E, tokens), bf16),
        pltpu.VMEM((L, tokens), bf16),
        pltpu.VMEM((tokens, L), bf16),
        pltpu.VMEM((tokens, L), bf16),
        pltpu.VMEM((tokens, L), bf16),
        pltpu.VMEM((tokens, tokens), bf16),
        pltpu.VMEM((EP, tokens), bf16),
        pltpu.VMEM((ns, EP, L), bf16),
        pltpu.VMEM((L, d), bf16),
        pltpu.VMEM((nc, L, width), bf16),
        pltpu.VMEM((L, width), bf16),
        pltpu.VMEM((nc, L, width), bf16),
        pltpu.VMEM((ns, EP, L), bf16),
        pltpu.VMEM((L, tokens), bf16),
        pltpu.VMEM((tokens, L), bf16),
        pltpu.VMEM((EP, tokens), f32),
        pltpu.VMEM((2 * E, tokens), bf16),
        pltpu.VMEM((EP, tokens), bf16),
        pltpu.VMEM((ns, 2 * E, L), bf16),
        pltpu.VMEM((ns, EP, L), bf16),
        pltpu.SemaphoreType.DMA((6, ns)),
        pltpu.SemaphoreType.DMA((6, ns)),
        pltpu.SemaphoreType.DMA((2, nc)),
        pltpu.SemaphoreType.DMA((2, nc)),
        pltpu.SemaphoreType.DMA((2,)),
    ]
    prediction, qkv_grad = pl.pallas_call(
        functools.partial(kernel, ns, nc),
        out_shape=(
            jax.ShapeDtypeStruct((1, 1, nc, L, width), bf16),
            jax.ShapeDtypeStruct((1, L, 3 * d), bf16),
        ),
        in_specs=[vmem, hbm, vmem, vmem, vmem, vmem, vmem, hbm],
        out_specs=(vmem, vmem),
        scratch_shapes=scratch,
        compiler_params=pltpu.CompilerParams(
            collective_id=0, has_side_effects=True, vmem_limit_bytes=56 * 1024 * 1024
        ),
        cost_estimate=pl.CostEstimate(flops=16_000_000_000, bytes_accessed=12_000_000, transcendentals=4_194_304),
    )(qkv, w_out, enc_gain[None], w_embed, pred_gain[None], ctx_blocks, owner[None], cotangent)
    return (prediction, qkv_grad)


def solution(mesh):
    placed = (
        P("clip", "seq", None),
        P(),
        P(),
        P(),
        P(),
        P(),
        P(),
        P("clip", "seq", None, None, None),
    )
    return jax.shard_map(
        functools.partial(on_device, mesh.shape["seq"], mesh.shape["clip"]),
        mesh=mesh,
        in_specs=placed,
        out_specs=(P("clip", "seq", None, None, None), P("clip", "seq", None)),
        check_vma=False,
    )
```

time: 307 us -> 110 us (0.36)
  waiting for transfers between devices: 150 us -> 0 us
  Pallas kernels: 0 us -> 102 us
  matrix products: 44.3 us -> 0 us
  starting transfers between devices: 35.3 us -> 0 us
  local copies, waits for them, and re-layouts: 42.4 us -> 7.86 us
  other arithmetic: 33.1 us -> 0 us
    all_to_all x6 -> x0, waiting for transfers between devices: 150 us -> none  [the longest x1 72.1 us: on_device(): lax.all_to_all(outgoing, 'clip', split_axis=0, concat_axis=0, tiled=True)]
    pallas_call x0 -> x1, Pallas kernels: none -> 102 us  [on_device(): pl.pallas_call(functools.partial(kernel, ns, nc), out_shape=(jax.ShapeDty...]
    dot_general x35 -> x0, matrix products: 44.3 us -> none  [the longest x4 7 us: one_block(): lax.dot_general(grad_block, value_rows, contract_last, preferred_element_...]
    all_to_all x6 -> x0, starting transfers between devices: 35.3 us -> none  [the longest x2 14.1 us: to_heads(): lax.all_to_all(token_rows.reshape(token_rows.shape[0], number, columns_ea...]
    unnamed x26 -> x5, local copies, waits for them, and re-layouts: 24.9 us -> 5.3 us
    another operation x7 -> x0, other arithmetic: 15.9 us -> none  [the longest x1 12.5 us: on_device(): heads_out = jnp.stack(outputs, axis=1).reshape(sequence, heads_here * E)]
    reduce_sum x16 -> x0, other arithmetic: 12.1 us -> none  [the longest x8 6.59 us: block_weights(): return shifted / jnp.sum(shifted, axis=-1, keepdims=True)]
    all_to_all x5 -> x0, local copies, waits for them, and re-layouts: 9.71 us -> none  [the longest x4 9.57 us: to_rows(): lax.all_to_all(head_columns.reshape(head_columns.shape[0], 1, head_column...]
  transfers between devices with their start and end apart: 6 -> 0, of which waited for: 5 -> 0; matrix products, arithmetic and copies ran while one was open for 17% -> 0% of each run, Pallas kernels for 0% -> 0%
where the time goes in v1:
time: 110 us
  Pallas kernels  102 us (93%)
  local copies, waits for them, and re-layouts  7.86 us (7%)
    pallas_call x1, Pallas kernels, on_device(): pl.pallas_call(functools.partial(kernel, ns, nc), out_shape=(jax.ShapeDty...  102 us
    unnamed x5, local copies, waits for them, and re-layouts  5.3 us

profile of v1, /device:TPU:1, one launch (start us, length us, event | category | flops | bytes accessed | tf_op | source)
XLA Modules:
  0.0 110.1 jit_solution(16743701875062154564)
XLA Ops:
  0.6 1.3 %broadcast_in_dim.10.pred_gain = f32[1,384]{1,0:T(1,128)} reshape(f32[384]{0:T(512)} %param.12) | data formatting | bytes 3072 | tf_op jit(solution)/shard_map/broadcast_in_dim | solution.py:441
  1.9 1.3 %broadcast_in_dim.9.enc_gain = f32[1,1408]{1,0:T(1,128)} reshape(f32[1408]{0:T(1024)} %param.10) | data formatting | bytes 11264 | tf_op jit(solution)/shard_map/broadcast_in_dim | solution.py:441
  3.2 1.5 %copy.10.ctx_blocks = s32[192,12]{1,0:T(8,128)} copy(s32[192,12]{0,1:T(8,128)} %param.13) | data formatting | bytes 18432 | tf_op args[5]
  4.7 101.6 %shard_map.95 = (bf16[1,1,16,128,384]{4,3,2,1,0:T(8,128)(2,1)}, bf16[1,128,4224]{2,1,0:T(8,128)(2,1)}) custom-call(bf16[1,128,4224]{2,1,0:T(8,128)(2,1)} %qkv.1, bf16[1408,1408]{1,0:T(8,128)(2,1)} %w_out_hbm.1, f32[1,1408]{1,0:T(1,128)} %broadcast_in_dim.9.enc_gain, bf16[1408,384]{1,0:T(8,128)(2,1)} %w_embed.1, f32[1,384]{1,0:T(1,128)} %broadcast_in_dim.10.pred_gain, ...), custom_call_target="tpu_custom_call" | custom-call | flops 16000000000 | bytes 12000000 | tf_op jit(solution)/shard_map/pallas_call | solution.py:428
  106.3 0.0 copy-start
  106.3 2.9 %copy.13 = bf16[1,1,16,128,384]{4,3,2,1,0:T(8,128)(2,1)} copy(bf16[1,1,16,128,384]{4,3,2,1,0:T(8,128)(2,1)} %get-tuple-element.4) | data formatting | bytes 3145728
  109.2 0.0 copy-done
  109.2 1.0 copy.14
Async XLA Ops:
  106.3 2.9 %copy-start = (bf16[1,128,4224]{2,1,0:T(8,128)(2,1)S(1)}, bf16[1,128,4224]{2,1,0:T(8,128)(2,1)}, u32[]{:S(2)}) copy-start(bf16[1,128,4224]{2,1,0:T(8,128)(2,1)} %get-tuple-element.5) | copy-start | bytes 3244036

commit v2 on v1

--- a/solution.py
+++ b/solution.py
@@ -52,18 +52,21 @@
 def kernel(
     ns,
     nc,
-    qkv,
+    qkv_hbm,
     w_out_hbm,
     enc_gain,
-    w_embed,
+    w_embed_hbm,
     pred_gain,
     ctx_blocks,
     owner,
     cot_hbm,
     prediction,
-    qkv_grad,
+    dkv_recv,
+    dq_recv,
     xt,
+    qkv,
     w_out,
+    w_embed,
     kv_send,
     q_send,
     kvt,
@@ -73,6 +76,9 @@
     qn,
     pt,
     ot,
+    score_rows,
+    inverse_total,
+    correction,
     heads_recv,
     heads_rows,
     cot_recv,
@@ -84,8 +90,7 @@
     dq,
     dkv_send,
     dq_send,
-    dkv_recv,
-    dq_recv,
+    pred_masked,
     seq_send_sem,
     seq_recv_sem,
     clip_send_sem,
@@ -99,6 +104,7 @@
     partner = me + 1 - 2 * lax.rem(me, 2)
     d = ns * E
     tiles = d // L
+    width = w_embed_hbm.shape[1]
     scaling = E**-0.5
     to_exp2 = scaling * 1.4426950408889634
 
@@ -145,6 +151,19 @@
     def seq_at(offset):
         return lax.rem(me + offset + ns, ns)
 
+    def pair_at(i, way=1):
+        ahead = (pairs // 2 - lax.div(i, 2)) * (1 - 2 * lax.rem(i, 2))
+        return lax.rem(my_pair + way * ahead + 2 * pairs, pairs)
+
+    def each_peer(body, way=1):
+        def both(i):
+            pair = pair_at(i, way)
+            body(2 * pair)
+            body(2 * pair + 1)
+
+        body(partner)
+        each(1, pairs, both)
+
     def clip_at(offset):
         return lax.rem(clip + offset + nc, nc)
 
@@ -155,55 +174,64 @@
 
         lax.fori_loop(first, last, step, 0)
 
+    qkv_in = []
+    for p in range(3):
+        columns = pl.ds(p * d, d)
+        qkv_in.append(pltpu.make_async_copy(qkv_hbm.at[0, :, columns], qkv.at[:, columns], local_sem.at[5 + p]))
+        qkv_in[-1].start()
+
     barrier = pltpu.get_barrier_semaphore()
     each(1, ns, lambda j: pl.semaphore_signal(barrier, inc=1, device_id={"seq": seq_at(j)}, device_id_type=MESH))
     each(1, nc, lambda j: pl.semaphore_signal(barrier, inc=1, device_id={"clip": clip_at(j)}, device_id_type=MESH))
 
     w_out_copy = pltpu.make_async_copy(w_out_hbm, w_out, local_sem.at[0])
     w_out_copy.start()
+    w_embed_copy = pltpu.make_async_copy(w_embed_hbm, w_embed, local_sem.at[8])
+    w_embed_copy.start()
     own_cot = pltpu.make_async_copy(cot_hbm.at[0, 0, clip], cot_recv.at[clip], local_sem.at[1])
     own_cot.start()
 
-    for j in range(3 * tiles):
-        xt[j * L : (j + 1) * L, :] = qkv[0, :, j * L : (j + 1) * L].astype(f32).T
-
-    def cut(h):
-        first = 3 * E * h
-        kv_send[h] = xt[pl.ds(pl.multiple_of(first + E, 8), 2 * E), :].astype(bf16)
-        q_send[h] = xt[pl.ds(pl.multiple_of(first, 8), EP), :].astype(bf16)
-
-    each(0, ns, cut)
+    for p in range(3):
+        qkv_in[p].wait()
+        for j in range(p * tiles, (p + 1) * tiles):
+            xt[j * L : (j + 1) * L, :] = qkv[:, j * L : (j + 1) * L].astype(f32).T
     pl.semaphore_wait(barrier, ns + nc - 2)
 
-    def send_kv(j):
-        peer = seq_at(j)
+    def kv_of(h):
+        return xt[pl.ds(pl.multiple_of(3 * E * h + E, 8), 2 * E), :].astype(bf16)
+
+    def q_of(h):
+        return xt[pl.ds(pl.multiple_of(3 * E * h, 8), EP), :].astype(bf16)
+
+    def send_kv(peer):
+        kv_send[peer] = kv_of(peer)
         seq_copy(KV, kv_send.at[peer], kvt.at[:, block(me)], peer).start()
 
-    def send_q(j):
-        peer = seq_at(j)
+    def send_q(peer):
+        q_send[peer] = q_of(peer)
         seq_copy(Q, q_send.at[peer], qt.at[pl.ds(0, EP), block(me)], peer).start()
 
     def send_cot(j):
         peer = clip_at(j)
         clip_copy(COT, cot_hbm.at[0, 0, peer], cot_recv.at[clip], peer).start()
 
-    each(1, ns, send_kv)
-    each(1, ns, send_q)
+    each_peer(send_kv, -1)
+    each_peer(send_q, -1)
     each(1, nc, send_cot)
 
-    kvt[:, block(me)] = kv_send[me]
-    qt[pl.ds(0, EP), block(me)] = q_send[me]
+    kvt[:, block(me)] = kv_of(me)
+    qt[pl.ds(0, EP), block(me)] = q_of(me)
     qt[pl.ds(EP, L - EP), :] = jnp.zeros((L - EP, ns * L), bf16)
     dot_t[pl.ds(EP, L - EP), :] = jnp.zeros((L - EP, ns * L), bf16)
     dq[...] = jnp.zeros_like(dq)
     masks = owner.shape[1]
     per_clip = masks // nc
     owned = (lax.broadcasted_iota(jnp.int32, (nc, masks), 0) == owner[...]).astype(f32)
-    member = jnp.max((ctx_blocks[...] == me).astype(f32), axis=1, keepdims=True)
+    member = jnp.max((ctx_blocks[...] == me).astype(f32), axis=0, keepdims=True)
     mask_id = lax.broadcasted_iota(jnp.int32, (masks, nc), 0)
     first_mask = lax.broadcasted_iota(jnp.int32, (masks, nc), 1) * per_clip
     in_clip = jnp.where((mask_id >= first_mask) & (mask_id < first_mask + per_clip), 1.0, 0.0)
-    table = dot(owned, member * in_clip)
+    table = dot(owned * member, in_clip)
     sending = jnp.sum(
         jnp.where(lax.broadcasted_iota(jnp.int32, (nc, nc), 1) == clip, table, 0.0), axis=1, keepdims=True
     )
@@ -230,12 +258,27 @@
 
     def attend(pair):
         columns = block(pair, 2 * L)
-        scores = dot(kn[...], qt[:, columns])
-        shifted = jnp.exp2((scores - jnp.max(scores, axis=0, keepdims=True)) * to_exp2)
-        probs = (shifted * (1.0 / jnp.sum(shifted, axis=0, keepdims=True))).astype(bf16)
-        pt[:, columns] = probs
-        mixed = dot(kvt[2 * E - EP :, :], probs)[EP - E :]
-        ot[:, columns] = rows_to(mixed, EP).astype(bf16)
+        queries = qt[:, columns]
+        largest = None
+        for k in range(pairs):
+            keys = slice(2 * L * k, 2 * L * (k + 1))
+            scores = dot(kn[keys, :], queries)
+            score_rows[keys, :] = scores
+            part = jnp.max(scores.reshape(2 * L // 8, 8, 2 * L), axis=0)
+            largest = part if largest is None else jnp.maximum(largest, part)
+        largest = jnp.max(largest, axis=0, keepdims=True)
+        total = jnp.zeros((8, 2 * L), f32)
+        mixed = jnp.zeros((EP, 2 * L), f32)
+        for k in range(pairs):
+            keys = slice(2 * L * k, 2 * L * (k + 1))
+            shifted = jnp.exp2((score_rows[keys, :] - largest) * to_exp2)
+            total += jnp.sum(shifted.reshape(2 * L // 8, 8, 2 * L), axis=0)
+            probs = shifted.astype(bf16)
+            pt[keys, columns] = probs
+            mixed += dot(kvt[2 * E - EP :, keys], probs)
+        inverse = 1.0 / jnp.sum(total, axis=0, keepdims=True)
+        inverse_total[:, columns] = inverse
+        ot[:, columns] = rows_to(mixed[EP - E :] * inverse, EP).astype(bf16)
 
     def wait_q(source):
         seq_wait(Q, qt.at[pl.ds(0, EP), block(source)], source)
@@ -251,7 +294,7 @@
     turn_q(partner)
 
     def attend_far(i):
-        pair = lax.rem(my_pair - i + pairs, pairs)
+        pair = pair_at(i)
         wait_q(2 * pair)
         wait_q(2 * pair + 1)
         attend(pair)
@@ -268,6 +311,7 @@
     for o in range(nc):
         grad_predicted += sending[o : o + 1, :] * cot_recv[o].astype(f32)
     w_out_copy.wait()
+    w_embed_copy.wait()
 
     def take_heads(j):
         source = seq_at(-j)
@@ -280,33 +324,37 @@
         heads_rows[:, j * L : (j + 1) * L] = xt[j * L : (j + 1) * L, :].T.astype(bf16)
     encoded = dot(heads_rows[...], w_out[...])
     normed_enc, inverse_enc = normalize(encoded)
-    context = (normed_enc * enc_gain[...]).astype(bf16)
+    context = (normed_enc * enc_gain[...].reshape(1, d)).astype(bf16)
     embedded = dot(context, w_embed[...])
     normed_emb, inverse_emb = normalize(embedded)
-    predicted = (normed_emb * pred_gain[...]).astype(bf16)
+    predicted = (normed_emb * pred_gain[...].reshape(1, width)).astype(bf16)
     pred_send[...] = predicted
 
     def send_pred(j):
         peer = clip_at(j)
         clip_copy(PRED, pred_send, pred_recv.at[clip], peer).start()
 
-    grad_embedded = norm_backward(normed_emb, inverse_emb, grad_predicted * pred_gain[...]).astype(bf16)
+    grad_embedded = norm_backward(normed_emb, inverse_emb, grad_predicted * pred_gain[...].reshape(1, width)).astype(bf16)
     grad_context = dot_last(grad_embedded, w_embed[...])
-    grad_encoded = norm_backward(normed_enc, inverse_enc, grad_context * enc_gain[...]).astype(bf16)
+    grad_encoded = norm_backward(normed_enc, inverse_enc, grad_context * enc_gain[...].reshape(1, d)).astype(bf16)
     xt[0:d, :] = dot_last(w_out[...], grad_encoded)
 
-    def cut_grads(j):
-        peer = seq_at(j)
+    def cut_grads(peer):
         grads_send[peer] = xt[pl.ds(pl.multiple_of(peer * E, 8), EP), :].astype(bf16)
         seq_copy(GRADS, grads_send.at[peer], dot_t.at[pl.ds(0, EP), block(me)], peer).start()
 
-    each(1, ns, cut_grads)
+    each_peer(cut_grads)
     each(1, nc, send_pred)
     dot_t[pl.ds(0, EP), block(me)] = xt[pl.ds(pl.multiple_of(me * E, 8), EP), :].astype(bf16)
     pred_recv[clip] = predicted
 
     def turn_grads(source):
-        dot_n[block(source), :] = dot_t[:, block(source)].astype(f32).T.astype(bf16)
+        rounded = (dot_t[:, block(source)].astype(f32) * inverse_total[:, block(source)]).astype(bf16)
+        dot_t[:, block(source)] = rounded
+        scaled = rounded.astype(f32)
+        dot_n[block(source), :] = scaled.T.astype(bf16)
+        mixed = ot[:, block(source)].astype(f32)
+        correction[:, block(source)] = jnp.sum(scaled[:EP] * mixed, axis=0, keepdims=True)
 
     turn_grads(me)
 
@@ -317,13 +365,11 @@
 
     each(1, ns, take_grads)
 
-    correction = jnp.sum(dot_t[0:EP, :].astype(f32) * ot[...].astype(f32), axis=0, keepdims=True)
-
     def backward(pair):
         rows = block(pair, 2 * L)
         probs = pt[rows, :]
         grad_probs = dot(vn[rows, :], dot_t[...])
-        grad_scores = (probs.astype(f32) * (grad_probs - correction)).astype(bf16)
+        grad_scores = (probs.astype(f32) * (grad_probs - correction[...])).astype(bf16)
         grad_value = dot(probs, dot_n[...])
         grad_key = dot(grad_scores, qn[...]) * scaling
         dq[...] += dot(kvt[0:EP, rows], grad_scores)
@@ -333,7 +379,7 @@
         seq_copy(DKV, dkv_send.at[:, block(peer)], dkv_recv.at[me], peer).start()
 
     def backward_far(i):
-        pair = lax.rem(my_pair + i, pairs)
+        pair = pair_at(i)
         backward(pair)
         send_dkv(2 * pair)
         send_dkv(2 * pair + 1)
@@ -341,19 +387,22 @@
     each(1, pairs, backward_far)
     backward(my_pair)
     send_dkv(partner)
-    dkv_recv[me] = dkv_send[:, block(me)]
+    own_dkv = pltpu.make_async_copy(dkv_send.at[:, block(me)], dkv_recv.at[me], local_sem.at[3])
+    own_dkv.start()
     dq_send[...] = (dq[...] * scaling).astype(bf16)
 
-    def send_dq(j):
-        peer = seq_at(j)
+    def send_dq(peer):
         seq_copy(DQ, dq_send.at[:, block(peer)], dq_recv.at[me], peer).start()
 
-    each(1, ns, send_dq)
-    dq_recv[me] = dq_send[:, block(me)]
+    each_peer(send_dq)
+    own_dq = pltpu.make_async_copy(dq_send.at[:, block(me)], dq_recv.at[me], local_sem.at[4])
+    own_dq.start()
 
     each(1, nc, lambda j: clip_wait(PRED, pred_recv.at[clip_at(-j)], clip_at(-j)))
     for c in range(nc):
-        prediction[0, 0, c] = (pred_recv[c].astype(f32) * receiving[:, c : c + 1]).astype(bf16)
+        pred_masked[c] = (pred_recv[c].astype(f32) * receiving[:, c : c + 1]).astype(bf16)
+    pred_copy = pltpu.make_async_copy(pred_masked, prediction, local_sem.at[2])
+    pred_copy.start()
 
     def take_grad(j):
         source = seq_at(-j)
@@ -361,15 +410,9 @@
         seq_wait(DQ, dq_recv.at[source], source)
 
     each(1, ns, take_grad)
-
-    def place(h):
-        first = 3 * E * h
-        xt[pl.ds(pl.multiple_of(first, 8), E), :] = dq_recv[h].astype(f32)[:E]
-        xt[pl.ds(pl.multiple_of(first + E, 8), 2 * E), :] = dkv_recv[h].astype(f32)
-
-    each(0, ns, place)
-    for j in range(3 * tiles):
-        qkv_grad[0, :, j * L : (j + 1) * L] = xt[j * L : (j + 1) * L, :].T.astype(bf16)
+    own_dkv.wait()
+    own_dq.wait()
+    pred_copy.wait()
 
     def sent(j):
         peer = seq_at(j)
@@ -389,6 +432,41 @@
     each(1, nc, sent_clip)
 
 
+def finish(ns, parts, masked_hbm, dkv_hbm, dq_hbm, prediction, qkv_grad, masked, dkv, dq, xt, turned, sems):
+    tiles = qkv_grad.shape[2] // L
+    thirds = tiles // 3
+    each_part = masked.shape[0] // parts
+    dkv_in = pltpu.make_async_copy(dkv_hbm, dkv, sems.at[0])
+    dq_in = pltpu.make_async_copy(dq_hbm, dq, sems.at[1])
+    dkv_in.start()
+    dq_in.start()
+    blocks_in, blocks_out = [], []
+    for p in range(parts):
+        some = pl.ds(p * each_part, each_part)
+        blocks_in.append(pltpu.make_async_copy(masked_hbm.at[some], masked.at[some], sems.at[2 + p]))
+        blocks_out.append(pltpu.make_async_copy(masked.at[some], prediction.at[0, 0, some], sems.at[2 + parts + p]))
+    for copy in blocks_in:
+        copy.start()
+    dkv_in.wait()
+    dq_in.wait()
+    for h in range(ns):
+        first = 3 * E * h
+        xt[first : first + E, :] = dq[h].astype(f32)[:E]
+        xt[first + E : first + 3 * E, :] = dkv[h].astype(f32)
+    grads_out = []
+    for p in range(3):
+        for j in range(p * thirds, (p + 1) * thirds):
+            turned[:, j * L : (j + 1) * L] = xt[j * L : (j + 1) * L, :].T.astype(bf16)
+        columns = pl.ds(p * thirds * L, thirds * L)
+        grads_out.append(pltpu.make_async_copy(turned.at[:, columns], qkv_grad.at[0, :, columns], sems.at[2 + 2 * parts + p]))
+        grads_out[-1].start()
+        for q in range(p * parts // 3, (p + 1) * parts // 3):
+            blocks_in[q].wait()
+            blocks_out[q].start()
+    for copy in blocks_out + grads_out:
+        copy.wait()
+
+
 def on_device(ns, nc, qkv, w_out, enc_gain, w_embed, pred_gain, ctx_blocks, owner, cotangent):
     d, width = w_embed.shape
     tokens = ns * L
@@ -396,7 +474,9 @@
     hbm = pl.BlockSpec(memory_space=pl.ANY)
     scratch = [
         pltpu.VMEM((3 * d + 16, L), f32),
+        pltpu.VMEM((L, 3 * d), bf16),
         pltpu.VMEM((d, d), bf16),
+        pltpu.VMEM((d, width), bf16),
         pltpu.VMEM((ns, 2 * E, L), bf16),
         pltpu.VMEM((ns, EP, L), bf16),
         pltpu.VMEM((2 * E, tokens), bf16),
@@ -406,6 +486,9 @@
         pltpu.VMEM((tokens, L), bf16),
         pltpu.VMEM((tokens, tokens), bf16),
         pltpu.VMEM((EP, tokens), bf16),
+        pltpu.VMEM((tokens, 2 * L), f32),
+        pltpu.VMEM((1, tokens), f32),
+        pltpu.VMEM((1, tokens), f32),
         pltpu.VMEM((ns, EP, L), bf16),
         pltpu.VMEM((L, d), bf16),
         pltpu.VMEM((nc, L, width), bf16),
@@ -417,29 +500,48 @@
         pltpu.VMEM((EP, tokens), f32),
         pltpu.VMEM((2 * E, tokens), bf16),
         pltpu.VMEM((EP, tokens), bf16),
-        pltpu.VMEM((ns, 2 * E, L), bf16),
-        pltpu.VMEM((ns, EP, L), bf16),
+        pltpu.VMEM((nc, L, width), bf16),
         pltpu.SemaphoreType.DMA((6, ns)),
         pltpu.SemaphoreType.DMA((6, ns)),
         pltpu.SemaphoreType.DMA((2, nc)),
         pltpu.SemaphoreType.DMA((2, nc)),
-        pltpu.SemaphoreType.DMA((2,)),
+        pltpu.SemaphoreType.DMA((9,)),
     ]
-    prediction, qkv_grad = pl.pallas_call(
+    prediction, dkv, dq = pl.pallas_call(
         functools.partial(kernel, ns, nc),
         out_shape=(
-            jax.ShapeDtypeStruct((1, 1, nc, L, width), bf16),
-            jax.ShapeDtypeStruct((1, L, 3 * d), bf16),
+            jax.ShapeDtypeStruct((nc, L, width), bf16),
+            jax.ShapeDtypeStruct((ns, 2 * E, L), bf16),
+            jax.ShapeDtypeStruct((ns, EP, L), bf16),
         ),
-        in_specs=[vmem, hbm, vmem, vmem, vmem, vmem, vmem, hbm],
-        out_specs=(vmem, vmem),
+        in_specs=[hbm, hbm, vmem, hbm, vmem, vmem, vmem, hbm],
+        out_specs=(hbm, hbm, hbm),
         scratch_shapes=scratch,
         compiler_params=pltpu.CompilerParams(
             collective_id=0, has_side_effects=True, vmem_limit_bytes=56 * 1024 * 1024
         ),
         cost_estimate=pl.CostEstimate(flops=16_000_000_000, bytes_accessed=12_000_000, transcendentals=4_194_304),
-    )(qkv, w_out, enc_gain[None], w_embed, pred_gain[None], ctx_blocks, owner[None], cotangent)
-    return (prediction, qkv_grad)
+    )(qkv, w_out, enc_gain, w_embed, pred_gain, ctx_blocks.T, owner[None], cotangent)
+    parts = min(nc, 4)
+    return pl.pallas_call(
+        functools.partial(finish, ns, parts),
+        out_shape=(
+            jax.ShapeDtypeStruct((1, 1, nc, L, width), bf16),
+            jax.ShapeDtypeStruct((1, L, 3 * d), bf16),
+        ),
+        in_specs=[hbm, hbm, hbm],
+        out_specs=(hbm, hbm),
+        scratch_shapes=[
+            pltpu.VMEM((nc, L, width), bf16),
+            pltpu.VMEM((ns, 2 * E, L), bf16),
+            pltpu.VMEM((ns, EP, L), bf16),
+            pltpu.VMEM((3 * d, L), f32),
+            pltpu.VMEM((L, 3 * d), bf16),
+            pltpu.SemaphoreType.DMA((5 + 2 * parts,)),
+        ],
+        compiler_params=pltpu.CompilerParams(vmem_limit_bytes=56 * 1024 * 1024),
+        cost_estimate=pl.CostEstimate(flops=0, bytes_accessed=6_000_000, transcendentals=0),
+    )(prediction, dkv, dq)
 
 
 def solution(mesh):

time: 110 us -> 96 us (0.87)
  local copies, waits for them, and re-layouts: 7.86 us -> 0 us
  Pallas kernels: 102 us -> 95.2 us
    pallas_call x1, Pallas kernels: 102 us -> 92.2 us  [on_device(): pl.pallas_call(functools.partial(kernel, ns, nc), out_shape=(jax.ShapeDty...]
    unnamed x5 -> x0, local copies, waits for them, and re-layouts: 5.3 us -> none
    pallas_call x0 -> x1, Pallas kernels: none -> 3.08 us  [on_device(): pl.pallas_call(functools.partial(finish, ns, parts), out_shape=(jax.Shape...]
    broadcast_in_dim x2 -> x0, local copies, waits for them, and re-layouts: 2.57 us -> none  [the longest x1 1.29 us: on_device(): enc_gain[None]]
where the time goes in v2:
time: 96 us; the launch traced here: 95.9 us
  Pallas kernels  95.2 us (99%)
    pallas_call x1, Pallas kernels, on_device(): pl.pallas_call(functools.partial(kernel, ns, nc), out_shape=(jax.ShapeDty...  92.2 us
    pallas_call x1, Pallas kernels, on_device(): pl.pallas_call(functools.partial(finish, ns, parts), out_shape=(jax.Shape...  3.08 us

profile of v2, /device:TPU:1, one launch (start us, length us, event | category | flops | bytes accessed | tf_op | source)
XLA Modules:
  0.0 95.9 jit_solution(14830721788467428000)
XLA Ops:
  0.6 92.2 %shard_map.95 = (bf16[16,128,384]{2,1,0:T(8,128)(2,1)}, bf16[16,176,128]{2,1,0:T(8,128)(2,1)}, bf16[16,96,128]{2,1,0:T(8,128)(2,1)}) custom-call(bf16[1,128,4224]{2,1,0:T(8,128)(2,1)} %qkv_hbm.1, bf16[1408,1408]{1,0:T(8,128)(2,1)} %w_out_hbm.1, f32[1408]{0:T(1024)} %enc_gain.1, bf16[1408,384]{1,0:T(8,128)(2,1)} %w_embed_hbm.1, f32[384]{0:T(512)} %pred_gain.1, ...), custom_call_target="tpu_custom_call" | custom-call | flops 16000000000 | bytes 12000000 | tf_op jit(solution)/shard_map/pallas_call | solution.py:510
  92.8 3.1 %shard_map.96 = (bf16[1,1,16,128,384]{4,3,2,1,0:T(8,128)(2,1)}, bf16[1,128,4224]{2,1,0:T(8,128)(2,1)}) custom-call(bf16[16,128,384]{2,1,0:T(8,128)(2,1)} %get-tuple-element.5.masked_hbm, bf16[16,176,128]{2,1,0:T(8,128)(2,1)} %get-tuple-element.6.dkv_hbm, bf16[16,96,128]{2,1,0:T(8,128)(2,1)} %get-tuple-element.7.dq_hbm), custom_call_target="tpu_custom_call" | custom-call | bytes 6000000 | tf_op jit(solution)/shard_map/pallas_call | solution.py:526

commit v3 on v2

--- a/solution.py
+++ b/solution.py
@@ -88,6 +88,8 @@
     dot_t,
     dot_n,
     dq,
+    dk_sum,
+    dv_sum,
     dkv_send,
     dq_send,
     pred_masked,
@@ -102,6 +104,8 @@
     pairs = ns // 2
     my_pair = lax.div(me, 2)
     partner = me + 1 - 2 * lax.rem(me, 2)
+    quads = ns // 4
+    my_quad = lax.div(me, 4)
     d = ns * E
     tiles = d // L
     width = w_embed_hbm.shape[1]
@@ -155,6 +159,19 @@
         ahead = (pairs // 2 - lax.div(i, 2)) * (1 - 2 * lax.rem(i, 2))
         return lax.rem(my_pair + way * ahead + 2 * pairs, pairs)
 
+    def place_of(source):
+        return block(lax.rem(source, 2) * pairs + lax.div(source, 2))
+
+    def quad_at(i):
+        ahead = jnp.where(i == 0, 0, (quads // 2 - lax.div(i, 2)) * (1 - 2 * lax.rem(i, 2)))
+        return lax.rem(my_quad + ahead + 2 * quads, quads)
+
+    def members(core, quad):
+        return 4 * quad + core, 4 * quad + 2 + core
+
+    def unless_me(source, body):
+        pl.when(source != me)(lambda: body(source))
+
     def each_peer(body, way=1):
         def both(i):
             pair = pair_at(i, way)
@@ -205,11 +222,11 @@
 
     def send_kv(peer):
         kv_send[peer] = kv_of(peer)
-        seq_copy(KV, kv_send.at[peer], kvt.at[:, block(me)], peer).start()
+        seq_copy(KV, kv_send.at[peer], kvt.at[:, place_of(me)], peer).start()
 
     def send_q(peer):
         q_send[peer] = q_of(peer)
-        seq_copy(Q, q_send.at[peer], qt.at[pl.ds(0, EP), block(me)], peer).start()
+        seq_copy(Q, q_send.at[peer], qt.at[pl.ds(0, EP), place_of(me)], peer).start()
 
     def send_cot(j):
         peer = clip_at(j)
@@ -219,11 +236,13 @@
     each_peer(send_q, -1)
     each(1, nc, send_cot)
 
-    kvt[:, block(me)] = kv_of(me)
-    qt[pl.ds(0, EP), block(me)] = q_of(me)
+    kvt[:, place_of(me)] = kv_of(me)
+    qt[pl.ds(0, EP), place_of(me)] = q_of(me)
     qt[pl.ds(EP, L - EP), :] = jnp.zeros((L - EP, ns * L), bf16)
     dot_t[pl.ds(EP, L - EP), :] = jnp.zeros((L - EP, ns * L), bf16)
     dq[...] = jnp.zeros_like(dq)
+    dk_sum[...] = jnp.zeros_like(dk_sum)
+    dv_sum[...] = jnp.zeros_like(dv_sum)
     masks = owner.shape[1]
     per_clip = masks // nc
     owned = (lax.broadcasted_iota(jnp.int32, (nc, masks), 0) == owner[...]).astype(f32)
@@ -240,21 +259,21 @@
     )
 
     def turn_kv(source):
-        both = kvt[:, block(source)].astype(f32)
-        kn[block(source), :] = rows_to(both[:E], L).T.astype(bf16)
-        vn[block(source), :] = rows_to(both[E:], L).T.astype(bf16)
+        both = kvt[:, place_of(source)].astype(f32)
+        kn[place_of(source), :] = rows_to(both[:E], L).T.astype(bf16)
+        vn[place_of(source), :] = rows_to(both[E:], L).T.astype(bf16)
 
     turn_kv(me)
 
     def take_kv(j):
         source = seq_at(-j)
-        seq_wait(KV, kvt.at[:, block(source)], source)
+        seq_wait(KV, kvt.at[:, place_of(source)], source)
         turn_kv(source)
 
     each(1, ns, take_kv)
 
     def turn_q(source):
-        qn[block(source), :] = qt[:, block(source)].astype(f32).T.astype(bf16)
+        qn[place_of(source), :] = qt[:, place_of(source)].astype(f32).T.astype(bf16)
 
     def attend(pair):
         columns = block(pair, 2 * L)
@@ -281,29 +300,32 @@
         ot[:, columns] = rows_to(mixed[EP - E :] * inverse, EP).astype(bf16)
 
     def wait_q(source):
-        seq_wait(Q, qt.at[pl.ds(0, EP), block(source)], source)
+        seq_wait(Q, qt.at[pl.ds(0, EP), place_of(source)], source)
 
     def send_heads(peer):
-        seq_copy(HEADS, ot.at[:, block(peer)], heads_recv.at[me], peer).start()
-
-    wait_q(partner)
-    attend(my_pair)
-    send_heads(partner)
-    heads_recv[me] = ot[:, block(me)]
-    turn_q(me)
-    turn_q(partner)
-
-    def attend_far(i):
-        pair = pair_at(i)
-        wait_q(2 * pair)
-        wait_q(2 * pair + 1)
-        attend(pair)
-        send_heads(2 * pair)
-        send_heads(2 * pair + 1)
-        turn_q(2 * pair)
-        turn_q(2 * pair + 1)
-
-    each(1, pairs, attend_far)
+        seq_copy(HEADS, ot.at[:, place_of(peer)], heads_recv.at[me], peer).start()
+
+    def keep_heads(source):
+        heads_recv[me] = ot[:, place_of(me)]
+
+    def attend_core(core):
+        def step(i):
+            quad = quad_at(i)
+            first, second = members(core, quad)
+            unless_me(first, wait_q)
+            unless_me(second, wait_q)
+            attend(core * quads + quad)
+            unless_me(first, send_heads)
+            unless_me(second, send_heads)
+            turn_q(first)
+            turn_q(second)
+
+        each(1, quads, step)
+        step(0 * me)
+
+    attend_core(0)
+    attend_core(1)
+    keep_heads(me)
 
     own_cot.wait()
     each(1, nc, lambda j: clip_wait(COT, cot_recv.at[clip_at(-j)], clip_at(-j)))
@@ -341,61 +363,103 @@
 
     def cut_grads(peer):
         grads_send[peer] = xt[pl.ds(pl.multiple_of(peer * E, 8), EP), :].astype(bf16)
-        seq_copy(GRADS, grads_send.at[peer], dot_t.at[pl.ds(0, EP), block(me)], peer).start()
+        seq_copy(GRADS, grads_send.at[peer], dot_t.at[pl.ds(0, EP), place_of(me)], peer).start()
 
     each_peer(cut_grads)
     each(1, nc, send_pred)
-    dot_t[pl.ds(0, EP), block(me)] = xt[pl.ds(pl.multiple_of(me * E, 8), EP), :].astype(bf16)
+    dot_t[pl.ds(0, EP), place_of(me)] = xt[pl.ds(pl.multiple_of(me * E, 8), EP), :].astype(bf16)
     pred_recv[clip] = predicted
 
     def turn_grads(source):
-        rounded = (dot_t[:, block(source)].astype(f32) * inverse_total[:, block(source)]).astype(bf16)
-        dot_t[:, block(source)] = rounded
+        rounded = (dot_t[:, place_of(source)].astype(f32) * inverse_total[:, place_of(source)]).astype(bf16)
+        dot_t[:, place_of(source)] = rounded
         scaled = rounded.astype(f32)
-        dot_n[block(source), :] = scaled.T.astype(bf16)
-        mixed = ot[:, block(source)].astype(f32)
-        correction[:, block(source)] = jnp.sum(scaled[:EP] * mixed, axis=0, keepdims=True)
-
-    turn_grads(me)
-
-    def take_grads(j):
-        source = seq_at(-j)
-        seq_wait(GRADS, dot_t.at[pl.ds(0, EP), block(source)], source)
+        dot_n[place_of(source), :] = scaled.T.astype(bf16)
+        mixed = ot[:, place_of(source)].astype(f32)
+        correction[:, place_of(source)] = jnp.sum(scaled[:EP] * mixed, axis=0, keepdims=True)
+
+    def take_grads(source):
+        def wait():
+            seq_wait(GRADS, dot_t.at[pl.ds(0, EP), place_of(source)], source)
+
+        pl.when(source != me)(wait)
         turn_grads(source)
 
-    each(1, ns, take_grads)
-
-    def backward(pair):
+    def send_dkv(peer):
+        seq_copy(DKV, dkv_send.at[:, place_of(peer)], dkv_recv.at[me], peer).start()
+
+    def send_dq(peer):
+        seq_copy(DQ, dq_send.at[:, place_of(peer)], dq_recv.at[me], peer).start()
+
+    def backward_queries(pair):
+        columns = block(pair, 2 * L)
+        grads_t, grads_n, queries = dot_t[:, columns], dot_n[columns, :], qn[columns, :]
+        shift = correction[:, columns]
+        grad_query = jnp.zeros((EP, 2 * L), f32)
+        for k in range(pairs):
+            keys = slice(2 * L * k, 2 * L * (k + 1))
+            probs = pt[keys, columns]
+            grad_probs = dot(vn[keys, :], grads_t)
+            grad_scores = (probs.astype(f32) * (grad_probs - shift)).astype(bf16)
+            grad_query += dot(kvt[0:EP, keys], grad_scores)
+            dv_sum[keys, :] += dot(probs, grads_n)
+            dk_sum[keys, :] += dot(grad_scores, queries)
+        dq_send[:, columns] = (grad_query * scaling).astype(bf16)
+
+    def first_core(i):
+        quad = quad_at(i)
+        first, second = members(0, quad)
+        take_grads(first)
+        take_grads(second)
+        backward_queries(quad)
+        unless_me(first, send_dq)
+        unless_me(second, send_dq)
+
+    each(1, quads, first_core)
+    first_core(0 * me)
+
+    def take_second(i):
+        quad = quad_at(i)
+        first, second = members(1, quad)
+        take_grads(first)
+        take_grads(second)
+
+    each(0, quads, take_second)
+    half = pairs * L
+
+    def backward_keys(pair):
         rows = block(pair, 2 * L)
-        probs = pt[rows, :]
-        grad_probs = dot(vn[rows, :], dot_t[...])
-        grad_scores = (probs.astype(f32) * (grad_probs - correction[...])).astype(bf16)
-        grad_value = dot(probs, dot_n[...])
-        grad_key = dot(grad_scores, qn[...]) * scaling
+        probs = pt[rows, half:]
+        grad_probs = dot(vn[rows, :], dot_t[:, half:])
+        grad_scores = (probs.astype(f32) * (grad_probs - correction[:, half:])).astype(bf16)
+        grad_value = dv_sum[rows, :] + dot(probs, dot_n[half:, :])
+        grad_key = (dk_sum[rows, :] + dot(grad_scores, qn[half:, :])) * scaling
         dq[...] += dot(kvt[0:EP, rows], grad_scores)
         dkv_send[:, rows] = jnp.concatenate([grad_key.T[:E], grad_value.T[:E]]).astype(bf16)
 
-    def send_dkv(peer):
-        seq_copy(DKV, dkv_send.at[:, block(peer)], dkv_recv.at[me], peer).start()
-
-    def backward_far(i):
-        pair = pair_at(i)
-        backward(pair)
-        send_dkv(2 * pair)
-        send_dkv(2 * pair + 1)
-
-    each(1, pairs, backward_far)
-    backward(my_pair)
-    send_dkv(partner)
-    own_dkv = pltpu.make_async_copy(dkv_send.at[:, block(me)], dkv_recv.at[me], local_sem.at[3])
+    def second_core(i):
+        quad = quad_at(i)
+        for core in range(2):
+            first, second = members(core, quad)
+            backward_keys(core * quads + quad)
+            unless_me(first, send_dkv)
+            unless_me(second, send_dkv)
+
+    each(1, quads, second_core)
+    second_core(0 * me)
+    dq_send[:, half:] = (dq[...] * scaling).astype(bf16)
+
+    def send_second(i):
+        quad = quad_at(i)
+        first, second = members(1, quad)
+        unless_me(first, send_dq)
+        unless_me(second, send_dq)
+
+    each(1, quads, send_second)
+    send_second(0 * me)
+    own_dkv = pltpu.make_async_copy(dkv_send.at[:, place_of(me)], dkv_recv.at[me], local_sem.at[3])
     own_dkv.start()
-    dq_send[...] = (dq[...] * scaling).astype(bf16)
-
-    def send_dq(peer):
-        seq_copy(DQ, dq_send.at[:, block(peer)], dq_recv.at[me], peer).start()
-
-    each_peer(send_dq)
-    own_dq = pltpu.make_async_copy(dq_send.at[:, block(me)], dq_recv.at[me], local_sem.at[4])
+    own_dq = pltpu.make_async_copy(dq_send.at[:, place_of(me)], dq_recv.at[me], local_sem.at[4])
     own_dq.start()
 
     each(1, nc, lambda j: clip_wait(PRED, pred_recv.at[clip_at(-j)], clip_at(-j)))
@@ -416,12 +480,12 @@
 
     def sent(j):
         peer = seq_at(j)
-        seq_copy(KV, kv_send.at[peer], kvt.at[:, block(me)], peer).wait_send()
-        seq_copy(Q, q_send.at[peer], qt.at[pl.ds(0, EP), block(me)], peer).wait_send()
-        seq_copy(HEADS, ot.at[:, block(peer)], heads_recv.at[me], peer).wait_send()
-        seq_copy(GRADS, grads_send.at[peer], dot_t.at[pl.ds(0, EP), block(me)], peer).wait_send()
-        seq_copy(DKV, dkv_send.at[:, block(peer)], dkv_recv.at[me], peer).wait_send()
-        seq_copy(DQ, dq_send.at[:, block(peer)], dq_recv.at[me], peer).wait_send()
+        seq_copy(KV, kv_send.at[peer], kvt.at[:, place_of(me)], peer).wait_send()
+        seq_copy(Q, q_send.at[peer], qt.at[pl.ds(0, EP), place_of(me)], peer).wait_send()
+        seq_copy(HEADS, ot.at[:, place_of(peer)], heads_recv.at[me], peer).wait_send()
+        seq_copy(GRADS, grads_send.at[peer], dot_t.at[pl.ds(0, EP), place_of(me)], peer).wait_send()
+        seq_copy(DKV, dkv_send.at[:, place_of(peer)], dkv_recv.at[me], peer).wait_send()
+        seq_copy(DQ, dq_send.at[:, place_of(peer)], dq_recv.at[me], peer).wait_send()
 
     def sent_clip(j):
         peer = clip_at(j)
@@ -497,7 +561,9 @@
         pltpu.VMEM((ns, EP, L), bf16),
         pltpu.VMEM((L, tokens), bf16),
         pltpu.VMEM((tokens, L), bf16),
-        pltpu.VMEM((EP, tokens), f32),
+        pltpu.VMEM((EP, tokens // 2), f32),
+        pltpu.VMEM((tokens, L), f32),
+        pltpu.VMEM((tokens, L), f32),
         pltpu.VMEM((2 * E, tokens), bf16),
         pltpu.VMEM((EP, tokens), bf16),
         pltpu.VMEM((nc, L, width), bf16),

time: 96 us -> 94.2 us (0.981)
  Pallas kernels: 95.2 us -> 93.3 us
    pallas_call x1, Pallas kernels: 92.2 us -> 90.2 us  [on_device(): pl.pallas_call(functools.partial(kernel, ns, nc), out_shape=(jax.ShapeDty...]
where the time goes in v3:
time: 94.2 us; the launch traced here: 94.1 us
  Pallas kernels  93.3 us (99%)
    pallas_call x1, Pallas kernels, on_device(): pl.pallas_call(functools.partial(kernel, ns, nc), out_shape=(jax.ShapeDty...  90.2 us
    pallas_call x1, Pallas kernels, on_device(): pl.pallas_call(functools.partial(finish, ns, parts), out_shape=(jax.Shape...  3.08 us

profile of v3, /device:TPU:1, one launch (start us, length us, event | category | flops | bytes accessed | tf_op | source)
XLA Modules:
  0.0 94.1 jit_solution(559468808351566915)
XLA Ops:
  0.6 90.2 %shard_map.95 = (bf16[16,128,384]{2,1,0:T(8,128)(2,1)}, bf16[16,176,128]{2,1,0:T(8,128)(2,1)}, bf16[16,96,128]{2,1,0:T(8,128)(2,1)}) custom-call(bf16[1,128,4224]{2,1,0:T(8,128)(2,1)} %qkv_hbm.1, bf16[1408,1408]{1,0:T(8,128)(2,1)} %w_out_hbm.1, f32[1408]{0:T(1024)} %enc_gain.1, bf16[1408,384]{1,0:T(8,128)(2,1)} %w_embed_hbm.1, f32[384]{0:T(512)} %pred_gain.1, ...), custom_call_target="tpu_custom_call" | custom-call | flops 16000000000 | bytes 12000000 | tf_op jit(solution)/shard_map/pallas_call | solution.py:576
  90.8 3.1 %shard_map.96 = (bf16[1,1,16,128,384]{4,3,2,1,0:T(8,128)(2,1)}, bf16[1,128,4224]{2,1,0:T(8,128)(2,1)}) custom-call(bf16[16,128,384]{2,1,0:T(8,128)(2,1)} %get-tuple-element.5.masked_hbm, bf16[16,176,128]{2,1,0:T(8,128)(2,1)} %get-tuple-element.6.dkv_hbm, bf16[16,96,128]{2,1,0:T(8,128)(2,1)} %get-tuple-element.7.dq_hbm), custom_call_target="tpu_custom_call" | custom-call | bytes 6000000 | tf_op jit(solution)/shard_map/pallas_call | solution.py:592

commit v4 on v3

--- a/solution.py
+++ b/solution.py
@@ -15,7 +15,7 @@
 bf16, f32 = jnp.bfloat16, jnp.float32
 contract_last = (((1,), (1,)), ((), ()))
 
-KV, Q, HEADS, GRADS, DKV, DQ = range(6)
+QK, V, HEADS, GRADS, DKV, DQ = range(6)
 COT, PRED = range(2)
 
 
@@ -67,9 +67,10 @@
     qkv,
     w_out,
     w_embed,
-    kv_send,
-    q_send,
-    kvt,
+    qk_send,
+    v_send,
+    qkt,
+    vt,
     qt,
     kn,
     vn,
@@ -98,6 +99,7 @@
     clip_send_sem,
     clip_recv_sem,
     local_sem,
+    ready,
 ):
     me = lax.axis_index("seq")
     clip = lax.axis_index("clip")
@@ -199,7 +201,11 @@
 
     barrier = pltpu.get_barrier_semaphore()
     each(1, ns, lambda j: pl.semaphore_signal(barrier, inc=1, device_id={"seq": seq_at(j)}, device_id_type=MESH))
-    each(1, nc, lambda j: pl.semaphore_signal(barrier, inc=1, device_id={"clip": clip_at(j)}, device_id_type=MESH))
+    each(
+        clip + 1,
+        nc,
+        lambda c: pl.semaphore_signal(barrier, inc=1, device_id={"clip": c}, device_id_type=MESH),
+    )
 
     w_out_copy = pltpu.make_async_copy(w_out_hbm, w_out, local_sem.at[0])
     w_out_copy.start()
@@ -212,33 +218,34 @@
         qkv_in[p].wait()
         for j in range(p * tiles, (p + 1) * tiles):
             xt[j * L : (j + 1) * L, :] = qkv[:, j * L : (j + 1) * L].astype(f32).T
-    pl.semaphore_wait(barrier, ns + nc - 2)
-
-    def kv_of(h):
-        return xt[pl.ds(pl.multiple_of(3 * E * h + E, 8), 2 * E), :].astype(bf16)
-
-    def q_of(h):
-        return xt[pl.ds(pl.multiple_of(3 * E * h, 8), EP), :].astype(bf16)
-
-    def send_kv(peer):
-        kv_send[peer] = kv_of(peer)
-        seq_copy(KV, kv_send.at[peer], kvt.at[:, place_of(me)], peer).start()
-
-    def send_q(peer):
-        q_send[peer] = q_of(peer)
-        seq_copy(Q, q_send.at[peer], qt.at[pl.ds(0, EP), place_of(me)], peer).start()
+    pl.semaphore_wait(barrier, ns - 1 + clip)
+    each(0, clip, lambda c: pl.semaphore_signal(ready, inc=1, device_id={"clip": c}, device_id_type=MESH))
+
+    xt[pl.ds(3 * d, 16), :] = jnp.zeros((16, L), f32)
+
+    def qk_of(h):
+        return xt[pl.ds(pl.multiple_of(3 * E * h, 8), 2 * E), :].astype(bf16)
+
+    def v_of(h):
+        return xt[pl.ds(pl.multiple_of(3 * E * h + 2 * E, 8), EP), :].astype(bf16)
+
+    def send_qk(peer):
+        qk_send[peer] = qk_of(peer)
+        seq_copy(QK, qk_send.at[peer], qkt.at[:, place_of(me)], peer).start()
+
+    def send_v(peer):
+        v_send[peer] = v_of(peer)
+        seq_copy(V, v_send.at[peer], vt.at[:, place_of(me)], peer).start()
 
     def send_cot(j):
         peer = clip_at(j)
         clip_copy(COT, cot_hbm.at[0, 0, peer], cot_recv.at[clip], peer).start()
 
-    each_peer(send_kv, -1)
-    each_peer(send_q, -1)
-    each(1, nc, send_cot)
-
-    kvt[:, place_of(me)] = kv_of(me)
-    qt[pl.ds(0, EP), place_of(me)] = q_of(me)
-    qt[pl.ds(EP, L - EP), :] = jnp.zeros((L - EP, ns * L), bf16)
+    each_peer(send_qk, -1)
+    each_peer(send_v, -1)
+
+    qkt[:, place_of(me)] = qk_of(me)
+    vt[:, place_of(me)] = v_of(me)
     dot_t[pl.ds(EP, L - EP), :] = jnp.zeros((L - EP, ns * L), bf16)
     dq[...] = jnp.zeros_like(dq)
     dk_sum[...] = jnp.zeros_like(dk_sum)
@@ -258,24 +265,27 @@
         jnp.where(lax.broadcasted_iota(jnp.int32, (nc, nc), 0) == clip, table, 0.0), axis=0, keepdims=True
     )
 
-    def turn_kv(source):
-        both = kvt[:, place_of(source)].astype(f32)
-        kn[place_of(source), :] = rows_to(both[:E], L).T.astype(bf16)
-        vn[place_of(source), :] = rows_to(both[E:], L).T.astype(bf16)
-
-    turn_kv(me)
-
-    def take_kv(j):
+    def turn_qk(source):
+        both = qkt[:, place_of(source)].astype(f32)
+        query, key = rows_to(both[:E], L), rows_to(both[E:], L)
+        qt[:, place_of(source)] = query.astype(bf16)
+        qn[place_of(source), :] = query.T.astype(bf16)
+        kn[place_of(source), :] = key.T.astype(bf16)
+
+    turn_qk(me)
+
+    def take_qk(j):
         source = seq_at(-j)
-        seq_wait(KV, kvt.at[:, place_of(source)], source)
-        turn_kv(source)
-
-    each(1, ns, take_kv)
-
-    def turn_q(source):
-        qn[place_of(source), :] = qt[:, place_of(source)].astype(f32).T.astype(bf16)
-
-    def attend(pair):
+        seq_wait(QK, qkt.at[:, place_of(source)], source)
+        turn_qk(source)
+
+    each(7, 10, take_qk)
+    pl.when(clip < nc - 1)(lambda: pl.semaphore_wait(ready, nc - 1 - clip))
+    each(1, nc, send_cot)
+    each(1, 7, take_qk)
+    each(10, ns, take_qk)
+
+    def weigh(pair, carry):
         columns = block(pair, 2 * L)
         queries = qt[:, columns]
         largest = None
@@ -287,45 +297,56 @@
             largest = part if largest is None else jnp.maximum(largest, part)
         largest = jnp.max(largest, axis=0, keepdims=True)
         total = jnp.zeros((8, 2 * L), f32)
-        mixed = jnp.zeros((EP, 2 * L), f32)
         for k in range(pairs):
             keys = slice(2 * L * k, 2 * L * (k + 1))
             shifted = jnp.exp2((score_rows[keys, :] - largest) * to_exp2)
             total += jnp.sum(shifted.reshape(2 * L // 8, 8, 2 * L), axis=0)
-            probs = shifted.astype(bf16)
-            pt[keys, columns] = probs
-            mixed += dot(kvt[2 * E - EP :, keys], probs)
-        inverse = 1.0 / jnp.sum(total, axis=0, keepdims=True)
-        inverse_total[:, columns] = inverse
-        ot[:, columns] = rows_to(mixed[EP - E :] * inverse, EP).astype(bf16)
-
-    def wait_q(source):
-        seq_wait(Q, qt.at[pl.ds(0, EP), place_of(source)], source)
+            pt[keys, columns] = shifted.astype(bf16)
+        inverse_total[:, columns] = 1.0 / jnp.sum(total, axis=0, keepdims=True)
+        return carry
+
+    lax.fori_loop(0, pairs, weigh, 0)
+
+    def wait_v(source):
+        seq_wait(V, vt.at[:, place_of(source)], source)
+
+    def turn_v(source):
+        vn[place_of(source), :] = rows_to(vt[:, place_of(source)].astype(f32)[:E], L).T.astype(bf16)
 
     def send_heads(peer):
         seq_copy(HEADS, ot.at[:, place_of(peer)], heads_recv.at[me], peer).start()
 
-    def keep_heads(source):
-        heads_recv[me] = ot[:, place_of(me)]
-
-    def attend_core(core):
+    def mix_core(core):
         def step(i):
             quad = quad_at(i)
             first, second = members(core, quad)
-            unless_me(first, wait_q)
-            unless_me(second, wait_q)
-            attend(core * quads + quad)
+            columns = block(core * quads + quad, 2 * L)
+            mixed = dot(vt[...], pt[:, columns])[:E] * inverse_total[:, columns]
+            ot[:, columns] = rows_to(mixed, EP).astype(bf16)
             unless_me(first, send_heads)
             unless_me(second, send_heads)
-            turn_q(first)
-            turn_q(second)
 
         each(1, quads, step)
         step(0 * me)
 
-    attend_core(0)
-    attend_core(1)
-    keep_heads(me)
+
+    def heads_sent(peer):
+        seq_copy(HEADS, ot.at[:, place_of(peer)], heads_recv.at[me], peer).wait_send()
+
+    def sent_core(first_i, last_i, core):
+        def step(i):
+            first, second = members(core, quad_at(i))
+            unless_me(first, heads_sent)
+            unless_me(second, heads_sent)
+
+        each(first_i, last_i, step)
+
+    each(1, ns, lambda j: wait_v(seq_at(-j)))
+    mix_core(0)
+    each(0, ns, turn_v)
+    sent_core(1, 1 + 3, 0)
+    mix_core(1)
+    heads_recv[me] = ot[:, place_of(me)]
 
     own_cot.wait()
     each(1, nc, lambda j: clip_wait(COT, cot_recv.at[clip_at(-j)], clip_at(-j)))
@@ -401,10 +422,10 @@
             probs = pt[keys, columns]
             grad_probs = dot(vn[keys, :], grads_t)
             grad_scores = (probs.astype(f32) * (grad_probs - shift)).astype(bf16)
-            grad_query += dot(kvt[0:EP, keys], grad_scores)
+            grad_query += dot(qkt[2 * E - EP :, keys], grad_scores)
             dv_sum[keys, :] += dot(probs, grads_n)
             dk_sum[keys, :] += dot(grad_scores, queries)
-        dq_send[:, columns] = (grad_query * scaling).astype(bf16)
+        dq_send[:, columns] = rows_to(grad_query[EP - E :] * scaling, EP).astype(bf16)
 
     def first_core(i):
         quad = quad_at(i)
@@ -434,7 +455,7 @@
         grad_scores = (probs.astype(f32) * (grad_probs - correction[:, half:])).astype(bf16)
         grad_value = dv_sum[rows, :] + dot(probs, dot_n[half:, :])
         grad_key = (dk_sum[rows, :] + dot(grad_scores, qn[half:, :])) * scaling
-        dq[...] += dot(kvt[0:EP, rows], grad_scores)
+        dq[...] += dot(qkt[2 * E - EP :, rows], grad_scores)
         dkv_send[:, rows] = jnp.concatenate([grad_key.T[:E], grad_value.T[:E]]).astype(bf16)
 
     def second_core(i):
@@ -447,7 +468,7 @@
 
     each(1, quads, second_core)
     second_core(0 * me)
-    dq_send[:, half:] = (dq[...] * scaling).astype(bf16)
+    dq_send[:, half:] = rows_to(dq[EP - E :, :] * scaling, EP).astype(bf16)
 
     def send_second(i):
         quad = quad_at(i)
@@ -468,32 +489,33 @@
     pred_copy = pltpu.make_async_copy(pred_masked, prediction, local_sem.at[2])
     pred_copy.start()
 
-    def take_grad(j):
-        source = seq_at(-j)
-        seq_wait(DKV, dkv_recv.at[source], source)
-        seq_wait(DQ, dq_recv.at[source], source)
-
-    each(1, ns, take_grad)
-    own_dkv.wait()
-    own_dq.wait()
-    pred_copy.wait()
-
-    def sent(j):
-        peer = seq_at(j)
-        seq_copy(KV, kv_send.at[peer], kvt.at[:, place_of(me)], peer).wait_send()
-        seq_copy(Q, q_send.at[peer], qt.at[pl.ds(0, EP), place_of(me)], peer).wait_send()
-        seq_copy(HEADS, ot.at[:, place_of(peer)], heads_recv.at[me], peer).wait_send()
-        seq_copy(GRADS, grads_send.at[peer], dot_t.at[pl.ds(0, EP), place_of(me)], peer).wait_send()
-        seq_copy(DKV, dkv_send.at[:, place_of(peer)], dkv_recv.at[me], peer).wait_send()
-        seq_copy(DQ, dq_send.at[:, place_of(peer)], dq_recv.at[me], peer).wait_send()
-
     def sent_clip(j):
         peer = clip_at(j)
         clip_copy(COT, cot_hbm.at[0, 0, peer], cot_recv.at[clip], peer).wait_send()
         clip_copy(PRED, pred_send, pred_recv.at[clip], peer).wait_send()
 
+    def sent(j):
+        peer = seq_at(j)
+        seq_copy(QK, qk_send.at[peer], qkt.at[:, place_of(me)], peer).wait_send()
+        seq_copy(V, v_send.at[peer], vt.at[:, place_of(me)], peer).wait_send()
+        seq_copy(GRADS, grads_send.at[peer], dot_t.at[pl.ds(0, EP), place_of(me)], peer).wait_send()
+        seq_copy(DKV, dkv_send.at[:, place_of(peer)], dkv_recv.at[me], peer).wait_send()
+        seq_wait(DKV, dkv_recv.at[peer], peer)
+
+    def last(j):
+        peer = seq_at(j)
+        seq_copy(DQ, dq_send.at[:, place_of(peer)], dq_recv.at[me], peer).wait_send()
+        seq_wait(DQ, dq_recv.at[peer], peer)
+
+    each(1, nc, sent_clip)
+    own_dkv.wait()
+    own_dq.wait()
+    pred_copy.wait()
+    sent_core(1 + 3, quads, 0)
+    sent_core(0, 1, 0)
+    sent_core(0, quads, 1)
     each(1, ns, sent)
-    each(1, nc, sent_clip)
+    each(1, ns, last)
 
 
 def finish(ns, parts, masked_hbm, dkv_hbm, dq_hbm, prediction, qkv_grad, masked, dkv, dq, xt, turned, sems):
@@ -544,6 +566,7 @@
         pltpu.VMEM((ns, 2 * E, L), bf16),
         pltpu.VMEM((ns, EP, L), bf16),
         pltpu.VMEM((2 * E, tokens), bf16),
+        pltpu.VMEM((EP, tokens), bf16),
         pltpu.VMEM((L, tokens), bf16),
         pltpu.VMEM((tokens, L), bf16),
         pltpu.VMEM((tokens, L), bf16),
@@ -572,6 +595,7 @@
         pltpu.SemaphoreType.DMA((2, nc)),
         pltpu.SemaphoreType.DMA((2, nc)),
         pltpu.SemaphoreType.DMA((9,)),
+        pltpu.SemaphoreType.REGULAR,
     ]
     prediction, dkv, dq = pl.pallas_call(
         functools.partial(kernel, ns, nc),

time: 94.2 us -> 90.4 us (0.960)
  Pallas kernels: 93.3 us -> 89.1 us
    pallas_call x1, Pallas kernels: 90.2 us -> 86 us  [on_device(): pl.pallas_call(functools.partial(kernel, ns, nc), out_shape=(jax.ShapeDty...]
where the time goes in v4:
time: 90.4 us; the launch traced here: 89.7 us
  Pallas kernels  89.1 us (99%)
    pallas_call x1, Pallas kernels, on_device(): pl.pallas_call(functools.partial(kernel, ns, nc), out_shape=(jax.ShapeDty...  86 us
    pallas_call x1, Pallas kernels, on_device(): pl.pallas_call(functools.partial(finish, ns, parts), out_shape=(jax.Shape...  3.08 us

profile of v4, /device:TPU:1, one launch (start us, length us, event | category | flops | bytes accessed | tf_op | source)
XLA Modules:
  0.0 89.7 jit_solution(769690720417890725)
XLA Ops:
  0.6 86.0 %shard_map.95 = (bf16[16,128,384]{2,1,0:T(8,128)(2,1)}, bf16[16,176,128]{2,1,0:T(8,128)(2,1)}, bf16[16,96,128]{2,1,0:T(8,128)(2,1)}) custom-call(bf16[1,128,4224]{2,1,0:T(8,128)(2,1)} %qkv_hbm.1, bf16[1408,1408]{1,0:T(8,128)(2,1)} %w_out_hbm.1, f32[1408]{0:T(1024)} %enc_gain.1, bf16[1408,384]{1,0:T(8,128)(2,1)} %w_embed_hbm.1, f32[384]{0:T(512)} %pred_gain.1, ...), custom_call_target="tpu_custom_call" | custom-call | flops 16000000000 | bytes 12000000 | tf_op jit(solution)/shard_map/pallas_call | solution.py:600
  86.6 3.1 %shard_map.96 = (bf16[1,1,16,128,384]{4,3,2,1,0:T(8,128)(2,1)}, bf16[1,128,4224]{2,1,0:T(8,128)(2,1)}) custom-call(bf16[16,128,384]{2,1,0:T(8,128)(2,1)} %get-tuple-element.5.masked_hbm, bf16[16,176,128]{2,1,0:T(8,128)(2,1)} %get-tuple-element.6.dkv_hbm, bf16[16,96,128]{2,1,0:T(8,128)(2,1)} %get-tuple-element.7.dq_hbm), custom_call_target="tpu_custom_call" | custom-call | bytes 6000000 | tf_op jit(solution)/shard_map/pallas_call | solution.py:616

commit v5 on v4

--- a/solution.py
+++ b/solution.py
@@ -518,38 +518,26 @@
     each(1, ns, last)
 
 
-def finish(ns, parts, masked_hbm, dkv_hbm, dq_hbm, prediction, qkv_grad, masked, dkv, dq, xt, turned, sems):
+def finish(ns, parts, masked, dkv, dq, prediction, qkv_grad, xt, turned, sems):
     tiles = qkv_grad.shape[2] // L
     thirds = tiles // 3
     each_part = masked.shape[0] // parts
-    dkv_in = pltpu.make_async_copy(dkv_hbm, dkv, sems.at[0])
-    dq_in = pltpu.make_async_copy(dq_hbm, dq, sems.at[1])
-    dkv_in.start()
-    dq_in.start()
-    blocks_in, blocks_out = [], []
+    copies = []
     for p in range(parts):
         some = pl.ds(p * each_part, each_part)
-        blocks_in.append(pltpu.make_async_copy(masked_hbm.at[some], masked.at[some], sems.at[2 + p]))
-        blocks_out.append(pltpu.make_async_copy(masked.at[some], prediction.at[0, 0, some], sems.at[2 + parts + p]))
-    for copy in blocks_in:
-        copy.start()
-    dkv_in.wait()
-    dq_in.wait()
+        copies.append(pltpu.make_async_copy(masked.at[some], prediction.at[0, 0, some], sems.at[p]))
+        copies[-1].start()
     for h in range(ns):
         first = 3 * E * h
         xt[first : first + E, :] = dq[h].astype(f32)[:E]
         xt[first + E : first + 3 * E, :] = dkv[h].astype(f32)
-    grads_out = []
     for p in range(3):
         for j in range(p * thirds, (p + 1) * thirds):
             turned[:, j * L : (j + 1) * L] = xt[j * L : (j + 1) * L, :].T.astype(bf16)
         columns = pl.ds(p * thirds * L, thirds * L)
-        grads_out.append(pltpu.make_async_copy(turned.at[:, columns], qkv_grad.at[0, :, columns], sems.at[2 + 2 * parts + p]))
-        grads_out[-1].start()
-        for q in range(p * parts // 3, (p + 1) * parts // 3):
-            blocks_in[q].wait()
-            blocks_out[q].start()
-    for copy in blocks_out + grads_out:
+        copies.append(pltpu.make_async_copy(turned.at[:, columns], qkv_grad.at[0, :, columns], sems.at[parts + p]))
+        copies[-1].start()
+    for copy in copies:
         copy.wait()
 
 
@@ -600,9 +588,9 @@
     prediction, dkv, dq = pl.pallas_call(
         functools.partial(kernel, ns, nc),
         out_shape=(
-            jax.ShapeDtypeStruct((nc, L, width), bf16),
-            jax.ShapeDtypeStruct((ns, 2 * E, L), bf16),
-            jax.ShapeDtypeStruct((ns, EP, L), bf16),
+            pltpu.VMEM((nc, L, width), bf16),
+            pltpu.VMEM((ns, 2 * E, L), bf16),
+            pltpu.VMEM((ns, EP, L), bf16),
         ),
         in_specs=[hbm, hbm, vmem, hbm, vmem, vmem, vmem, hbm],
         out_specs=(hbm, hbm, hbm),
@@ -619,17 +607,14 @@
             jax.ShapeDtypeStruct((1, 1, nc, L, width), bf16),
             jax.ShapeDtypeStruct((1, L, 3 * d), bf16),
         ),
-        in_specs=[hbm, hbm, hbm],
+        in_specs=[vmem, vmem, vmem],
         out_specs=(hbm, hbm),
         scratch_shapes=[
-            pltpu.VMEM((nc, L, width), bf16),
-            pltpu.VMEM((ns, 2 * E, L), bf16),
-            pltpu.VMEM((ns, EP, L), bf16),
             pltpu.VMEM((3 * d, L), f32),
             pltpu.VMEM((L, 3 * d), bf16),
-            pltpu.SemaphoreType.DMA((5 + 2 * parts,)),
+            pltpu.SemaphoreType.DMA((3 + parts,)),
         ],
-        compiler_params=pltpu.CompilerParams(vmem_limit_bytes=56 * 1024 * 1024),
+        compiler_params=pltpu.CompilerParams(vmem_limit_bytes=14 * 1024 * 1024),
         cost_estimate=pl.CostEstimate(flops=0, bytes_accessed=6_000_000, transcendentals=0),
     )(prediction, dkv, dq)
 

time: 90.4 us -> 88.7 us (0.981)
  Pallas kernels: 89.1 us -> 87.4 us
    pallas_call x1, Pallas kernels: 3.08 us -> 1.55 us  [on_device(): pl.pallas_call(functools.partial(finish, ns, parts), out_shape=(jax.Shape...]
where the time goes in v5:
time: 88.7 us; the launch traced here: 88 us
  Pallas kernels  87.4 us (99%)
    pallas_call x1, Pallas kernels, on_device(): pl.pallas_call(functools.partial(kernel, ns, nc), out_shape=(pltpu.VMEM((...  85.9 us

profile of v5, /device:TPU:1, one launch (start us, length us, event | category | flops | bytes accessed | tf_op | source)
XLA Modules:
  0.0 88.0 jit_solution(1199495168061004814)
XLA Ops:
  0.6 85.9 %shard_map.95 = (bf16[16,128,384]{2,1,0:T(8,128)(2,1)S(1)}, bf16[16,176,128]{2,1,0:T(8,128)(2,1)S(1)}, bf16[16,96,128]{2,1,0:T(8,128)(2,1)S(1)}) custom-call(bf16[1,128,4224]{2,1,0:T(8,128)(2,1)} %qkv_hbm.1, bf16[1408,1408]{1,0:T(8,128)(2,1)} %w_out_hbm.1, f32[1408]{0:T(1024)} %enc_gain.1, bf16[1408,384]{1,0:T(8,128)(2,1)} %w_embed_hbm.1, f32[384]{0:T(512)} %pred_gain.1, ...), custom_call_target="tpu_custom_call" | custom-call | flops 16000000000 | bytes 12000000 | tf_op jit(solution)/shard_map/pallas_call | solution.py:588
  86.5 1.6 %shard_map.96 = (bf16[1,1,16,128,384]{4,3,2,1,0:T(8,128)(2,1)}, bf16[1,128,4224]{2,1,0:T(8,128)(2,1)}) custom-call(bf16[16,128,384]{2,1,0:T(8,128)(2,1)S(1)} %get-tuple-element.5.masked, bf16[16,176,128]{2,1,0:T(8,128)(2,1)S(1)} %get-tuple-element.6.dkv, bf16[16,96,128]{2,1,0:T(8,128)(2,1)S(1)} %get-tuple-element.7.dq), custom_call_target="tpu_custom_call" | custom-call | bytes 6000000 | tf_op jit(solution)/shard_map/pallas_call | solution.py:604

commit v6 on v5

--- a/solution.py
+++ b/solution.py
@@ -476,8 +476,8 @@
         unless_me(first, send_dq)
         unless_me(second, send_dq)
 
+    send_second(0 * me)
     each(1, quads, send_second)
-    send_second(0 * me)
     own_dkv = pltpu.make_async_copy(dkv_send.at[:, place_of(me)], dkv_recv.at[me], local_sem.at[3])
     own_dkv.start()
     own_dq = pltpu.make_async_copy(dq_send.at[:, place_of(me)], dq_recv.at[me], local_sem.at[4])

time: 88.7 us -> 88.5 us (level)
  no operation moved by 1% of the time
where the time goes in v6:
time: 88.5 us; the launch traced here: 88 us
  Pallas kernels  87.4 us (99%)
    pallas_call x1, Pallas kernels, on_device(): pl.pallas_call(functools.partial(kernel, ns, nc), out_shape=(pltpu.VMEM((...  85.8 us

profile of v6, /device:TPU:1, one launch (start us, length us, event | category | flops | bytes accessed | tf_op | source)
XLA Modules:
  0.0 88.0 jit_solution(17474115426910851785)
XLA Ops:
  0.6 85.8 %shard_map.95 = (bf16[16,128,384]{2,1,0:T(8,128)(2,1)S(1)}, bf16[16,176,128]{2,1,0:T(8,128)(2,1)S(1)}, bf16[16,96,128]{2,1,0:T(8,128)(2,1)S(1)}) custom-call(bf16[1,128,4224]{2,1,0:T(8,128)(2,1)} %qkv_hbm.1, bf16[1408,1408]{1,0:T(8,128)(2,1)} %w_out_hbm.1, f32[1408]{0:T(1024)} %enc_gain.1, bf16[1408,384]{1,0:T(8,128)(2,1)} %w_embed_hbm.1, f32[384]{0:T(512)} %pred_gain.1, ...), custom_call_target="tpu_custom_call" | custom-call | flops 16000000000 | bytes 12000000 | tf_op jit(solution)/shard_map/pallas_call | solution.py:588
  86.5 1.6 %shard_map.96 = (bf16[1,1,16,128,384]{4,3,2,1,0:T(8,128)(2,1)}, bf16[1,128,4224]{2,1,0:T(8,128)(2,1)}) custom-call(bf16[16,128,384]{2,1,0:T(8,128)(2,1)S(1)} %get-tuple-element.5.masked, bf16[16,176,128]{2,1,0:T(8,128)(2,1)S(1)} %get-tuple-element.6.dkv, bf16[16,96,128]{2,1,0:T(8,128)(2,1)S(1)} %get-tuple-element.7.dq), custom_call_target="tpu_custom_call" | custom-call | bytes 6000000 | tf_op jit(solution)/shard_map/pallas_call | solution.py:604

commit v7 on v6

--- a/solution.py
+++ b/solution.py
@@ -93,7 +93,6 @@
     dv_sum,
     dkv_send,
     dq_send,
-    pred_masked,
     seq_send_sem,
     seq_recv_sem,
     clip_send_sem,
@@ -485,9 +484,7 @@
 
     each(1, nc, lambda j: clip_wait(PRED, pred_recv.at[clip_at(-j)], clip_at(-j)))
     for c in range(nc):
-        pred_masked[c] = (pred_recv[c].astype(f32) * receiving[:, c : c + 1]).astype(bf16)
-    pred_copy = pltpu.make_async_copy(pred_masked, prediction, local_sem.at[2])
-    pred_copy.start()
+        prediction[c] = (pred_recv[c].astype(f32) * receiving[:, c : c + 1]).astype(bf16)
 
     def sent_clip(j):
         peer = clip_at(j)
@@ -510,7 +507,6 @@
     each(1, nc, sent_clip)
     own_dkv.wait()
     own_dq.wait()
-    pred_copy.wait()
     sent_core(1 + 3, quads, 0)
     sent_core(0, 1, 0)
     sent_core(0, quads, 1)
@@ -577,7 +573,6 @@
         pltpu.VMEM((tokens, L), f32),
         pltpu.VMEM((2 * E, tokens), bf16),
         pltpu.VMEM((EP, tokens), bf16),
-        pltpu.VMEM((nc, L, width), bf16),
         pltpu.SemaphoreType.DMA((6, ns)),
         pltpu.SemaphoreType.DMA((6, ns)),
         pltpu.SemaphoreType.DMA((2, nc)),
@@ -593,7 +588,7 @@
             pltpu.VMEM((ns, EP, L), bf16),
         ),
         in_specs=[hbm, hbm, vmem, hbm, vmem, vmem, vmem, hbm],
-        out_specs=(hbm, hbm, hbm),
+        out_specs=(vmem, vmem, vmem),
         scratch_shapes=scratch,
         compiler_params=pltpu.CompilerParams(
             collective_id=0, has_side_effects=True, vmem_limit_bytes=56 * 1024 * 1024

time: 88.5 us -> 88.5 us (level)
  no operation moved by 1% of the time
where the time goes in v7:
time: 88.5 us; the launch traced here: 88 us
  Pallas kernels  87.4 us (99%)
    pallas_call x1, Pallas kernels, on_device(): pl.pallas_call(functools.partial(kernel, ns, nc), out_shape=(pltpu.VMEM((...  85.8 us

profile of v7, /device:TPU:1, one launch (start us, length us, event | category | flops | bytes accessed | tf_op | source)
XLA Modules:
  0.0 88.0 jit_solution(10367666884146143274)
XLA Ops:
  0.6 85.8 %shard_map.95 = (bf16[16,128,384]{2,1,0:T(8,128)(2,1)S(1)}, bf16[16,176,128]{2,1,0:T(8,128)(2,1)S(1)}, bf16[16,96,128]{2,1,0:T(8,128)(2,1)S(1)}) custom-call(bf16[1,128,4224]{2,1,0:T(8,128)(2,1)} %qkv_hbm.1, bf16[1408,1408]{1,0:T(8,128)(2,1)} %w_out_hbm.1, f32[1408]{0:T(1024)} %enc_gain.1, bf16[1408,384]{1,0:T(8,128)(2,1)} %w_embed_hbm.1, f32[384]{0:T(512)} %pred_gain.1, ...), custom_call_target="tpu_custom_call" | custom-call | flops 16000000000 | bytes 12000000 | tf_op jit(solution)/shard_map/pallas_call | solution.py:583
  86.5 1.6 %shard_map.96 = (bf16[1,1,16,128,384]{4,3,2,1,0:T(8,128)(2,1)}, bf16[1,128,4224]{2,1,0:T(8,128)(2,1)}) custom-call(bf16[16,128,384]{2,1,0:T(8,128)(2,1)S(1)} %get-tuple-element.5.masked, bf16[16,176,128]{2,1,0:T(8,128)(2,1)S(1)} %get-tuple-element.6.dkv, bf16[16,96,128]{2,1,0:T(8,128)(2,1)S(1)} %get-tuple-element.7.dq), custom_call_target="tpu_custom_call" | custom-call | bytes 6000000 | tf_op jit(solution)/shard_map/pallas_call | solution.py:599
